TPU v7x, 256 devices: a whole 4x4x8 slice. The times are simulated.
256 devices in a mesh: level: 4 (over z_lo), seq: 16 (over y, z_hi, core), dp: 4 (over x).
Axes of the slice: x: 4, y: 4, z: 8 (z_hi: 2, z_lo: 4; z = z_hi * 4 + z_lo), core: 2. Of those that a mesh axis runs over, the one named last changes fastest.
Arguments:
- feats: bfloat16 [4, 512, 5120], P('dp'), may hold values from -6 to 6
- gen_gain: float32 [5120], replicated, may hold values from 0.25 to 1.75
- gen_weight: bfloat16 [5120, 64], replicated, may hold values from -0.078125 to 0.078125
- noise: float32 [4, 4, 512, 64], P('level', 'dp'), may hold values from -6 to 6
- sigmas: float32 [4], P('level'), may hold values from 0.1 to 10
- level_weights: float32 [4], P('level'), may hold values from 0.3 to 3
- embed: bfloat16 [2, 64, 5120], replicated, may hold values from -0.75 to 0.75
- proj_in: bfloat16 [2, 3, 5120, 4096], P(None, None, ('level', 'dp'), 'seq'), may hold values from -0.078125 to 0.078125
- proj_out: bfloat16 [2, 4096, 5120], P(None, 'seq', ('level', 'dp')), may hold values from -0.09375 to 0.09375
- head_out: bfloat16 [2, 5120, 64], replicated, may hold values from -0.078125 to 0.078125
- qk_gain: float32 [2, 2, 128], replicated, may hold values from 0.5 to 2.5
Outputs:
- grad_h: bfloat16 [4, 512, 5120], P('dp', 'seq')
- grad_weight: float32 [5120, 64], P('dp')
- grad_gain: float32 [5120], P('dp')
All inputs are finite; a program needn't handle non-finite values.
Results may differ from a plain program's by a relative error of at most 0.019.
Values may be sent and summed in bfloat16 or wider, within the bound.
A program may use at most 192 MiB of HBM per device.

v0:
```python
import math

import jax
import jax.numpy as jnp
from jax import lax
from jax.sharding import PartitionSpec as P

HD = 128


def split_up(array, dim, count):
    before, after = (array.shape[:dim], array.shape[dim + 1 :])
    return jnp.moveaxis(array.reshape(*before, count, -1, *after), dim, 0)


def summed_on_arrival(array, axis, dim):
    blocks = split_up(array, dim, lax.axis_size(axis))
    arrived = lax.all_to_all(blocks, axis, split_axis=0, concat_axis=0, tiled=True)
    return arrived.sum(axis=0)


def from_everyone(array, axis):
    count = lax.axis_size(axis)
    return lax.all_to_all(
        jnp.broadcast_to(array[None], (count, *array.shape)), axis, 0, 0, tiled=True
    )


def of_everyone(array, axis):
    return from_everyone(array, axis).sum(axis=0)


def summed_on_arrival_2(array, axis, dim):
    blocks = split_up(array, dim, lax.axis_size(axis))
    arrived = lax.all_to_all(blocks, axis, split_axis=0, concat_axis=0, tiled=True)
    return arrived.astype(jnp.float32).sum(axis=0)


def in_one_piece(arrays, axis, dim, along):
    columns = [a.reshape(*a.shape[:along], -1) for a in arrays]
    both = jnp.concatenate(columns, axis=along)
    result, at, finished = (summed_on_arrival_2(both, axis, dim), 0, [])
    for a, column in zip(arrays, columns):
        section = result[..., at : at + column.shape[along]]
        finished.append(section.reshape(*section.shape[:along], *a.shape[along:]))
        at += column.shape[along]
    return tuple(finished)


def shape_heads(acts, gains, count):
    active = jax.nn.silu(acts)
    active = active.reshape(active.shape[0], 3, active.shape[2], count, HD)
    paired = active[:, :2]
    paired = paired * lax.rsqrt(jnp.mean(paired * paired, axis=-1, keepdims=True) + 1e-06)
    paired = paired * gains[:, :, None, None, :]
    return jnp.concatenate([paired, active[:, 2:]], axis=1).astype(jnp.bfloat16)


def attend_heads(qkv):
    queries, keys, values = (qkv[:, 0], qkv[:, 1], qkv[:, 2])
    span = queries.shape[1]
    count = queries.shape[2]
    size = min(512, span)
    blocks = span // size
    split = queries.reshape(2, blocks, size, count, HD).transpose(1, 0, 2, 3, 4)
    factor = 1.0 / math.sqrt(HD)

    def one_block(piece):
        scores = (
            jnp.einsum("nqhd,nkhd->nhqk", piece, keys, preferred_element_type=jnp.float32) * factor
        )
        scores = scores - jnp.max(scores, axis=-1, keepdims=True)
        weights = jnp.exp(scores)
        weights = (weights / jnp.sum(weights, axis=-1, keepdims=True)).astype(jnp.bfloat16)
        return jnp.einsum(
            "nhqk,nkhd->nqhd", weights, values, preferred_element_type=jnp.float32
        ).astype(jnp.bfloat16)

    outputs = lax.map(one_block, split)
    return outputs.transpose(1, 0, 2, 3, 4).reshape(2, span, count, HD)


def on_device(
    feats,
    gen_gain,
    gen_weight,
    noise,
    sigmas,
    level_weights,
    embed,
    proj_in,
    proj_out,
    head_out,
    qk_gain,
):
    span = feats.shape[1]
    ways = lax.axis_size("seq")
    rows = span // ways
    first_row = lax.axis_index("seq") * rows
    hidden = feats[0].astype(jnp.float32)
    rms = lax.rsqrt(jnp.mean(hidden * hidden, axis=-1, keepdims=True) + 1e-06)
    normed = hidden * rms
    u_mat = (normed * gen_gain).astype(jnp.bfloat16)
    x_zero = jnp.dot(u_mat, gen_weight, preferred_element_type=jnp.float32)
    width = proj_in.shape[3]
    own_heads = width // HD
    channels = gen_weight.shape[1]
    sigma = sigmas[0]
    noisy = ((x_zero + sigma * noise[0, 0]) * lax.rsqrt(sigma * sigma + 1.0)).astype(jnp.bfloat16)
    states = jnp.einsum("sc,ncd->nsd", noisy, embed, preferred_element_type=jnp.float32).astype(
        jnp.bfloat16
    )
    own_states = lax.dynamic_slice_in_dim(states, first_row, rows, 1)
    acts = jnp.einsum(
        "nsd,njdw->njsw",
        states,
        lax.all_gather(proj_in, ("level", "dp"), axis=2, tiled=True),
        preferred_element_type=jnp.float32,
    )
    qkv = shape_heads(acts, qk_gain, own_heads)
    attended = attend_heads(qkv)
    flat = attended.reshape(2, span, width)
    middle = jnp.einsum(
        "nsw,nwd->nsd",
        flat,
        lax.all_gather(proj_out, ("level", "dp"), axis=2, tiled=True),
        preferred_element_type=jnp.float32,
    )
    head_rows = head_out.astype(jnp.float32)
    partial_value = jnp.einsum("nsd,ndc->nsc", middle, head_rows, precision=lax.Precision.HIGHEST)
    arranged = partial_value.transpose(1, 0, 2).reshape(span, 2 * channels)
    summed = summed_on_arrival(arranged, "seq", 0)
    residual = jnp.einsum("nsd,ndc->nsc", own_states, head_out, preferred_element_type=jnp.float32)
    fields = summed.reshape(rows, 2, channels).transpose(1, 0, 2) + residual
    total = level_weights[0] * (fields[1] - fields[0])
    factor = 1.0 / math.sqrt(lax.axis_size("dp") * span)
    own_u = lax.dynamic_slice_in_dim(u_mat, first_row, rows, 0)
    own_norm = lax.dynamic_slice_in_dim(normed, first_row, rows, 0)
    own_rms = lax.dynamic_slice_in_dim(rms, first_row, rows, 0)
    g_low = of_everyone(total, "level").astype(jnp.bfloat16)
    part_u, part_norm, part_rms = (own_u, own_norm, own_rms)
    d_u = jnp.dot(g_low, gen_weight.T, preferred_element_type=jnp.float32)
    d_norm = d_u * gen_gain
    inner = jnp.mean(d_norm * part_norm, axis=-1, keepdims=True)
    grad_part = (part_rms * (d_norm - part_norm * inner)).astype(jnp.bfloat16)
    weight_term = jnp.dot(part_u.T, g_low, preferred_element_type=jnp.float32)
    gain_term = jnp.sum(d_u * part_norm, axis=0)
    sums = (
        lax.psum(weight_term.astype(jnp.bfloat16), "seq").astype(jnp.float32),
        lax.psum(gain_term.astype(jnp.bfloat16), "seq").astype(jnp.float32),
    )
    weight_part, gain_part = in_one_piece(
        (sums[0].astype(jnp.bfloat16), sums[1].astype(jnp.bfloat16)), "dp", 0, 1
    )
    return (grad_part[None], weight_part * factor, gain_part * factor)


def solution(mesh):
    in_specs = (
        P("dp", None, None),
        P(),
        P(),
        P("level", "dp", None, None),
        P("level"),
        P("level"),
        P(),
        P(None, None, ("level", "dp"), "seq"),
        P(None, "seq", ("level", "dp")),
        P(),
        P(),
    )
    out_specs = (P("dp", "seq", None), P("dp", None), P("dp"))
    return jax.shard_map(
        on_device, mesh=mesh, in_specs=in_specs, out_specs=out_specs, check_vma=False
    )
```

profile of v0, /device:TPU:1, one launch (start us, length us, event | category | flops | bytes accessed | tf_op | source)
XLA Modules:
  0.0 537.7 jit_solution(2887063930938966364)
XLA Ops:
  7.2 0.0 copy-start
  7.2 0.0 copy-start.7
  7.2 0.0 all-gather.3.cloned.1.call-start
  7.2 0.7 all-gather.3.cloned.1.call-update
  7.9 0.0 all-gather.5.cloned.1.call-start
  8.0 0.7 all-gather.5.cloned.1.call-update
  9.4 0.0 copy-start.2
  9.4 0.8 copy.43
  10.2 3.8 fusion.1
  14.0 0.0 copy-done.7
  14.0 0.0 copy-done.2
  14.0 0.0 copy-start.5
  14.0 0.0 copy-start.8
  14.0 7.7 %multiply_convert_fusion = (bf16[512,5120]{1,0:T(8,128)(2,1)}, f32[512,5120]{1,0:T(8,128)}) fusion(f32[5120]{0:T(1024)S(1)} %copy-done.7, f32[512]{0:T(512)S(1)} %add_rsqrt_fusion.1, bf16[1,512,5120]{2,1,0:T(8,128)(2,1)S(1)} %copy-done.2), kind=kLoop, calls=%fused_computation.6 | loop fusion | flops 10485760 | bytes 20994048 | tf_op jit(solution)/shard_map/convert_element_type | solution.py:103
  21.7 0.0 copy-done
  21.7 0.0 copy-done.5
  21.7 0.0 copy-done.8
  21.7 11.5 %convolution_convert_fusion = bf16[512,2,5120]{2,0,1:T(8,128)(2,1)} fusion(bf16[2,64,5120]{2,1,0:T(8,128)(2,1)S(1)} %copy-done, bf16[512,5120]{1,0:T(8,128)(2,1)} %get-tuple-element.20, bf16[5120,64]{0,1:T(8,128)(2,1)S(1)} %copy-done.5, f32[1,1,512,64]{2,3,1,0:T(8,128)S(1)} %copy-done.8, f32[]{:T(128)S(6)} %rsqrt.25, f32[]{:T(128)} %bitcast.89), kind=kOutput, calls=%fused_computation.7 | convolution fusion | flops 1012006912 | bytes 17825800 | tf_op jit(solution)/shard_map/sc,ncd->nsd/dot_general | solution.py:110
  33.2 156.6 %all-gather.3.cloned.1.call-done = bf16[2,3,5120,256]{3,2,1,0:T(8,128)(2,1)} async-done(((bf16[2,3,320,256]{3,2,1,0:T(8,128)(2,1)}), bf16[2,3,5120,256]{3,2,1,0:T(8,128)(2,1)}) %all-gather.3.cloned.1.call-update) | async-done | bytes 15728656 | tf_op jit(solution)/shard_map/all_gather | solution.py:117
  189.8 15.0 %bitcast_multiply_fusion = f32[2,3,512,256]{2,3,1,0:T(8,128)} fusion(bf16[2,3,5120,256]{3,2,1,0:T(8,128)(2,1)} %all-gather.3.cloned.1.call-done, bf16[512,2,5120]{2,0,1:T(8,128)(2,1)} %convolution_convert_fusion), kind=kOutput, calls=%fused_computation.13 | convolution fusion | flops 8056209408 | bytes 29360128 | tf_op jit(solution)/shard_map/nsd,njdw->njsw/dot_general | solution.py:114
  204.8 3.1 slice.37
  207.8 1.9 copy.53
  209.8 0.6 multiply_reduce_fusion.1
  210.4 0.7 multiply_convert_fusion.1
  211.1 0.7 fusion.22
  211.8 0.0 copy-start.4
  211.9 1.9 copy-done.4
  213.8 1.1 fusion.41
  214.9 5.3 fusion.14
  220.2 49.8 %all-gather.5.cloned.1.call-done = bf16[2,256,5120]{1,2,0:T(8,128)(2,1)} async-done(((bf16[2,256,320]{1,2,0:T(8,128)(2,1)}), bf16[2,256,5120]{1,2,0:T(8,128)(2,1)}) %all-gather.5.cloned.1.call-update) | async-done | bytes 5242896 | tf_op jit(solution)/shard_map/all_gather | solution.py:126
  270.0 0.0 copy-start.3
  270.0 11.2 %fusion.42 = f32[2,512,5120]{2,1,0:T(8,128)} fusion(bf16[2,512,256]{1,2,0:T(8,128)(2,1)S(1)} %bitcast.97, bf16[2,256,5120]{1,2,0:T(8,128)(2,1)} %all-gather.5.cloned.1.call-done), kind=kOutput, calls=%fused_computation.62 | convolution fusion | flops 2684354560 | bytes 26738688 | tf_op jit(solution)/shard_map/nsw,nwd->nsd/dot_general | solution.py:123
  281.2 0.0 copy-done.3
  281.2 15.1 %convolution_bitcast_fusion = f32[512,2,64]{0,2,1:T(8,128)S(1)} fusion(f32[2,512,5120]{2,1,0:T(8,128)} %fusion.42, bf16[2,5120,64]{1,2,0:T(8,128)(2,1)S(1)} %copy-done.3), kind=kOutput, calls=%fused_computation.24 | convolution fusion | flops 4026531840 | bytes 22544384 | tf_op jit(solution)/shard_map/nsd,ndc->nsc/dot_general | solution.py:130
  296.3 0.0 copy-start.6
  296.3 0.2 copy.46
  296.5 1.0 reshape_reshape.3
  297.6 17.2 %all-to-all-start = ((f32[16,32,128]{2,1,0:T(8,128)}), f32[16,32,128]{2,1,0:T(8,128)S(1)}, u32[]{:S(2)}, u32[]{:S(2)}) async-start(f32[16,32,128]{2,1,0:T(8,128)} %reshape_reshape.3), calls=%async_computation | async-start | bytes 524288 | tf_op jit(solution)/shard_map/all_to_all | solution.py:18
  314.8 0.0 all-reduce.2.cloned.1.call-start
  315.5 10.4 %all-to-all-done = f32[16,32,128]{2,1,0:T(8,128)S(1)} async-done(((f32[16,32,128]{2,1,0:T(8,128)}), f32[16,32,128]{2,1,0:T(8,128)S(1)}, u32[]{:S(2)}, u32[]{:S(2)}) %all-to-all-start) | async-done | bytes 262176 | tf_op jit(solution)/shard_map/all_to_all | solution.py:18
  325.9 0.1 reshape.66
  326.0 1.6 convolution_add_fusion.1
  327.6 0.1 reshape.71
  327.7 6.9 %all_to_all.15 = f32[4,1,2048]{2,1,0:T(1,128)S(1)} all-to-all(f32[4,1,2048]{2,1,0:T(1,128)S(1)} %reshape.71), channel_id=1, replica_groups=mesh['level'=4,'seq'=16,'dp'=4] {'level'}, dimensions={0} | all-to-all | bytes 65536 | tf_op jit(solution)/shard_map/all_to_all | solution.py:24
  334.5 0.5 broadcast.69
  335.0 0.7 reduce.2
  335.8 0.1 reshape.72
  335.9 1.4 convolution_convert_fusion.1
  337.3 0.9 copy.62
  338.1 0.0 all-reduce.2.cloned.1.call-update
  338.2 0.1 dynamic-slice.6
  338.2 0.0 copy-start.1
  338.2 0.0 copy-done.6
  338.2 1.6 multiply_reduce_fusion.2
  339.8 78.2 %psum.15 = bf16[4,1280,1]{1,0,2:T(4,128)(2,1)S(1)} all-reduce(bf16[4,1280,1]{1,0,2:T(4,128)(2,1)S(1)} %concatenate.11), channel_id=1, replica_groups=mesh['level'=4,'seq'=16,'dp'=4] {'seq'}, use_global_device_ids=true, to_apply=%region_9.10 | all-reduce | flops 5120 | bytes 20480 | tf_op jit(solution)/shard_map/psum | solution.py:150
  418.1 94.8 %all-reduce.2.cloned.1.call-done = bf16[4,1280,64]{1,2,0:T(8,128)(2,1)} async-done(((bf16[4,1280,64]{1,2,0:T(8,128)(2,1)}), bf16[4,1280,64]{1,2,0:T(8,128)(2,1)}) %all-reduce.2.cloned.1.call-update) | async-done | bytes 655376 | tf_op jit(solution)/shard_map/psum | solution.py:149
  512.9 2.0 pad_maximum_fusion
  515.0 4.0 all-to-all-start.2
  518.9 2.0 fusion.23
  520.9 8.8 %all-to-all-done.2 = bf16[4,1280,65]{1,2,0:T(8,128)(2,1)S(1)} async-done(((bf16[4,1280,65]{1,2,0:T(8,128)(2,1)}), bf16[4,1280,65]{1,2,0:T(8,128)(2,1)S(1)}, u32[]{:S(2)}, u32[]{:S(2)}) %all-to-all-start.2) | async-done | bytes 665632 | tf_op jit(solution)/shard_map/all_to_all | solution.py:35
  529.7 0.1 convert_reduce_fusion
  529.8 0.6 fusion.31
  530.4 0.8 slice_multiply_fusion
  531.2 0.0 copy-done.1
  (9 shorter events, 0.1 us)
Async XLA Ops:
  7.2 14.5 %copy-start = (bf16[2,64,5120]{2,1,0:T(8,128)(2,1)S(1)}, bf16[2,64,5120]{2,1,0:T(8,128)(2,1)}, u32[]{:S(2)}) copy-start(bf16[2,64,5120]{2,1,0:T(8,128)(2,1)} %param.17) | copy-start | bytes 3932164
  7.2 6.8 %copy-start.7 = (f32[5120]{0:T(1024)S(1)}, f32[5120]{0:T(1024)}, u32[]{:S(2)}) copy-start(f32[5120]{0:T(1024)} %param.12) | copy-start | bytes 61444
  7.2 182.6 %all-gather.3.cloned.1.call-start = ((), (), s32[]{:S(2)}) async-start(), calls=%async_computation.3 | async-start | bytes 16711680 | tf_op jit(solution)/shard_map/all_gather | solution.py:117
  7.9 262.0 %all-gather.5.cloned.1.call-start = ((), (), s32[]{:S(2)}) async-start(), calls=%async_computation.4 | async-start | bytes 5570560 | tf_op jit(solution)/shard_map/all_gather | solution.py:126
  9.4 4.6 copy-start.2
  14.0 7.7 %copy-start.5 = (bf16[5120,64]{0,1:T(8,128)(2,1)S(1)}, bf16[5120,64]{0,1:T(8,128)(2,1)}, u32[]{:S(2)}) copy-start(bf16[5120,64]{0,1:T(8,128)(2,1)} %param.13) | copy-start | bytes 1966084
  14.0 7.7 %copy-start.8 = (f32[1,1,512,64]{2,3,1,0:T(8,128)S(1)}, f32[1,1,512,64]{2,3,1,0:T(8,128)}, u32[]{:S(2)}) copy-start(f32[1,1,512,64]{2,3,1,0:T(8,128)} %param.14) | copy-start | bytes 393220
  211.8 1.9 copy-start.4
  270.0 11.2 %copy-start.3 = (bf16[2,5120,64]{1,2,0:T(8,128)(2,1)S(1)}, bf16[2,5120,64]{1,2,0:T(8,128)(2,1)}, u32[]{:S(2)}) copy-start(bf16[2,5120,64]{1,2,0:T(8,128)(2,1)} %param.20) | copy-start | bytes 3932164
  296.3 42.0 %copy-start.6 = (bf16[5120,64]{0,1:T(8,128)(2,1)S(1)}, bf16[5120,64]{0,1:T(8,128)(2,1)}, u32[]{:S(2)}) copy-start(bf16[5120,64]{0,1:T(8,128)(2,1)} %param.13) | copy-start | bytes 1966084
  297.6 28.3 %all-to-all-start = ((f32[16,32,128]{2,1,0:T(8,128)}), f32[16,32,128]{2,1,0:T(8,128)S(1)}, u32[]{:S(2)}, u32[]{:S(2)}) async-start(f32[16,32,128]{2,1,0:T(8,128)} %reshape_reshape.3), calls=%async_computation | async-start | bytes 524288 | tf_op jit(solution)/shard_map/all_to_all | solution.py:18
  314.8 198.2 %all-reduce.2.cloned.1.call-start = ((), (), s32[]{:S(2)}) async-start(), calls=%async_computation.5 | async-start | bytes 1310720 | tf_op jit(solution)/shard_map/psum | solution.py:149
  338.2 193.0 %copy-start.1 = (bf16[2,64,5120]{2,1,0:T(8,128)(2,1)S(1)}, bf16[2,64,5120]{2,1,0:T(8,128)(2,1)}, u32[]{:S(2)}) copy-start(bf16[2,64,5120]{2,1,0:T(8,128)(2,1)} %param.17) | copy-start | bytes 3932164
  515.0 14.8 %all-to-all-start.2 = ((bf16[4,1280,65]{1,2,0:T(8,128)(2,1)}), bf16[4,1280,65]{1,2,0:T(8,128)(2,1)S(1)}, u32[]{:S(2)}, u32[]{:S(2)}) async-start(bf16[4,1280,65]{1,2,0:T(8,128)(2,1)} %pad_maximum_fusion), calls=%async_computation.2 | async-start | bytes 1474560 | tf_op jit(solution)/shard_map/all_to_all | solution.py:35
Sparse Core Ops, SparseCore 0:
  9.8 179.9 all-gather.2
  191.6 78.3 all-gather.4
  338.3 174.6 all-reduce.1
where the time goes:
time: 538 us
  waiting for transfers between devices  322 us (60%)
  blocking collectives  85.1 us (16%)
  matrix products  63.3 us (12%)
  starting transfers between devices  21.3 us (4%)
  other arithmetic  20.1 us (4%)
  between operations  15.3 us (3%)
  local copies, waits for them, and re-layouts  10.8 us (2%)
    all_gather x1, waiting for transfers between devices, on_device(): lax.all_gather(proj_in, ('level', 'dp'), axis=2, tiled=True)  157 us
    psum x1, waiting for transfers between devices, on_device(): lax.psum(weight_term.astype(jnp.bfloat16), 'seq').astype(jnp.float32)  94.8 us
    psum x1, blocking collectives, on_device(): lax.psum(gain_term.astype(jnp.bfloat16), 'seq').astype(jnp.float32)  78.2 us
    all_gather x1, waiting for transfers between devices, on_device(): lax.all_gather(proj_out, ('level', 'dp'), axis=2, tiled=True)  49.8 us
    all_to_all x1, starting transfers between devices, summed_on_arrival(): lax.all_to_all(blocks, axis, split_axis=0, concat_axis=0, tiled=True)  17.2 us
    dot_general x1, matrix products, on_device(): jnp.einsum('nsd,ndc->nsc', middle, head_rows, precision=lax.Precision.HIG...  15.1 us
    dot_general x1, matrix products, on_device(): jnp.einsum('nsd,njdw->njsw', states, lax.all_gather(proj_in, ('level', 'd...  15 us
    dot_general x1, matrix products, on_device(): jnp.einsum('sc,ncd->nsd', noisy, embed, preferred_element_type=jnp.float32)  11.5 us
  transfers between devices with their start and end apart: 5, of which 5 were waited for; matrix products, arithmetic and copies ran while one was open for 10% of the time, Pallas kernels for 0%

commit v1 on v0

v1 whole, which is shorter than its diff:
```python
import math

import jax
import jax.numpy as jnp
from jax import lax
from jax.sharding import PartitionSpec as P

HD = 128
BF = jnp.bfloat16
F32 = jnp.float32


def on_device(feats, gen_gain, gen_weight, noise, sigmas, level_weights, embed, proj_in, proj_out, head_out, qk_gain):
    span, width_d = feats.shape[1:]
    ways = lax.axis_size("seq")
    rows = span // ways
    chans = gen_weight.shape[1]
    seq = lax.axis_index("seq")
    first_row = seq * rows
    part = proj_in.shape[2]
    spot = (lax.axis_index("level") * lax.axis_size("dp") + lax.axis_index("dp")) * part
    heads = proj_in.shape[3] // HD

    emb = lax.dynamic_slice_in_dim(embed, spot, part, 2)
    head = lax.dynamic_slice_in_dim(head_out, spot, part, 1)
    entry = jnp.einsum("ncd,njdw->njcw", emb, proj_in, preferred_element_type=F32)
    leave = jnp.einsum("nwd,ndc->ncw", proj_out, head, preferred_element_type=F32)
    fused = jnp.concatenate([entry, leave[:, None]], axis=1).astype(BF)
    fused = lax.psum(fused, ("level", "dp")).astype(BF)

    hidden = feats[0]
    wide = hidden.astype(F32)
    rms = lax.rsqrt(jnp.mean(wide * wide, axis=-1, keepdims=True) + 1e-06)
    scaled = (gen_weight.astype(F32) * gen_gain[:, None]).astype(BF)
    x_zero = jnp.dot(hidden, scaled, preferred_element_type=F32) * rms
    sigma = sigmas[0]
    xin = ((x_zero + sigma * noise[0, 0]) * lax.rsqrt(sigma * sigma + 1.0)).astype(BF)

    acts = jax.nn.silu(jnp.einsum("sc,njcw->njsw", xin, fused[:, :3], preferred_element_type=F32))
    acts = acts.reshape(2, 3, span, heads, HD)
    paired = acts[:, :2]
    paired = paired * lax.rsqrt(jnp.mean(paired * paired, axis=-1, keepdims=True) + 1e-06)
    paired = (paired * qk_gain[:, :, None, None, :]).astype(BF)
    values = acts[:, 2].astype(BF)
    scores = jnp.einsum("nqhd,nkhd->nhqk", paired[:, 0], paired[:, 1], preferred_element_type=F32)
    weights = jnp.exp(scores * (1.0 / math.sqrt(HD)))
    weights = (weights / jnp.sum(weights, axis=-1, keepdims=True)).astype(BF)
    outs = jnp.einsum("nhqk,nkhd->nqhd", weights, values, preferred_element_type=F32).astype(BF)
    outs = outs.reshape(2, span, heads * HD)
    field = jnp.einsum("nsw,ncw->nsc", outs, fused[:, 3], preferred_element_type=F32)
    part_s = width_d // ways
    emb_s = lax.dynamic_slice_in_dim(embed, seq * part_s, part_s, 2)
    head_s = lax.dynamic_slice_in_dim(head_out, seq * part_s, part_s, 1)
    straight = jnp.einsum("ncd,nde->nce", emb_s, head_s, preferred_element_type=F32)
    straight = (straight[1] - straight[0]).astype(BF)
    total = field[1] - field[0] + jnp.dot(xin, straight, preferred_element_type=F32)
    total = (level_weights[0] * total).reshape(span // 2, 2 * chans)
    total = lax.psum(total, ("level", "seq")).reshape(span, chans)
    g_low = total.astype(BF)

    term = jnp.einsum("sc,sd->cd", (g_low.astype(F32) * rms).astype(BF), hidden, preferred_element_type=F32)
    wsum = lax.psum_scatter(term.astype(BF), "dp", scatter_dimension=1, tiled=True).astype(F32)
    cut = width_d // lax.axis_size("dp")
    at = lax.axis_index("dp") * cut
    gain_cut = lax.dynamic_slice_in_dim(gen_gain, at, cut, 0)
    weight_cut = lax.dynamic_slice_in_dim(gen_weight, at, cut, 0).astype(F32)
    wsum = wsum.T * (1.0 / math.sqrt(lax.axis_size("dp") * span))
    grad_gain = jnp.sum(wsum * weight_cut, axis=1)
    grad_weight = wsum * gain_cut[:, None]

    own = lambda a: lax.dynamic_slice_in_dim(a, first_row, rows, 0)
    own_g, own_rms = own(g_low), own(rms)
    inner = jnp.sum(own_g.astype(F32) * own(x_zero), axis=-1, keepdims=True) / width_d
    d_norm = jnp.dot(own_g, gen_weight.T, preferred_element_type=F32) * gen_gain
    grad_h = (own_rms * (d_norm - own(wide) * own_rms * inner)).astype(BF)
    return (grad_h[None], grad_weight, grad_gain)


def solution(mesh):
    in_specs = (
        P("dp", None, None),
        P(),
        P(),
        P("level", "dp", None, None),
        P("level"),
        P("level"),
        P(),
        P(None, None, ("level", "dp"), "seq"),
        P(None, "seq", ("level", "dp")),
        P(),
        P(),
    )
    out_specs = (P("dp", "seq", None), P("dp", None), P("dp"))
    return jax.shard_map(on_device, mesh=mesh, in_specs=in_specs, out_specs=out_specs, check_vma=False)
```

time: 538 us -> 527 us (0.980)
  blocking collectives: 85.1 us -> 297 us
  waiting for transfers between devices: 322 us -> 166 us
  matrix products: 63.3 us -> 22.1 us
  starting transfers between devices: 21.3 us -> 0.08 us
    psum x1, blocking collectives: 78.2 us -> 297 us  [on_device(): total = lax.psum(total, ('level', 'seq')).reshape(span, chans)]
    all_gather x2 -> x0, waiting for transfers between devices: 206 us -> none  [the longest x1 157 us: on_device(): lax.all_gather(proj_in, ('level', 'dp'), axis=2, tiled=True)]
    psum x1, waiting for transfers between devices: 94.8 us -> 141 us  [on_device(): fused = lax.psum(fused, ('level', 'dp')).astype(BF)]
    dot_general x9 -> x11, matrix products: 63.3 us -> 22.1 us  [the longest x1 4.86 us: on_device(): x_zero = jnp.dot(hidden, scaled, preferred_element_type=F32) * rms]
    reduce_scatter x0 -> x1, waiting for transfers between devices: none -> 24.7 us  [on_device(): lax.psum_scatter(term.astype(BF), 'dp', scatter_dimension=1, tiled=True)]
    all_to_all x2 -> x0, starting transfers between devices: 21.2 us -> none  [the longest x1 17.2 us: summed_on_arrival(): lax.all_to_all(blocks, axis, split_axis=0, concat_axis=0, tiled=True)]
    all_to_all x2 -> x0, waiting for transfers between devices: 19.2 us -> none  [the longest x1 10.4 us: summed_on_arrival(): lax.all_to_all(blocks, axis, split_axis=0, concat_axis=0, tiled=True)]
    all_to_all x1 -> x0, blocking collectives: 6.86 us -> none  [from_everyone(): lax.all_to_all(jnp.broadcast_to(array[None], (count, *array.shape)), axis...]
  transfers between devices with their start and end apart: 5 -> 2, of which waited for: 5 -> 2; matrix products, arithmetic and copies ran while one was open for 10% -> 4% of each run, Pallas kernels for 0% -> 0%
where the time goes in v1:
time: 527 us; the launch traced here: 525 us
  blocking collectives  297 us (56%)
  waiting for transfers between devices  166 us (31%)
  matrix products  22.1 us (4%)
  other arithmetic  17.8 us (3%)
  between operations  15.7 us (3%)
  local copies, waits for them, and re-layouts  6.88 us (1%)
    psum x1, blocking collectives, on_device(): total = lax.psum(total, ('level', 'seq')).reshape(span, chans)  297 us
    psum x1, waiting for transfers between devices, on_device(): fused = lax.psum(fused, ('level', 'dp')).astype(BF)  141 us
    reduce_scatter x1, waiting for transfers between devices, on_device(): lax.psum_scatter(term.astype(BF), 'dp', scatter_dimension=1, tiled=True)  24.7 us
  transfers between devices with their start and end apart: 2, of which 2 were waited for; matrix products, arithmetic and copies ran while one was open for 4% of the time, Pallas kernels for 0%

profile of v1, /device:TPU:1, one launch (start us, length us, event | category | flops | bytes accessed | tf_op | source)
XLA Modules:
  0.0 525.4 jit_solution(15382273134232571425)
XLA Ops:
  7.2 0.0 copy-start
  7.2 0.0 all-reduce.3.cloned.1.call-start
  7.2 1.4 fusion.18
  8.6 0.0 copy-done
  8.6 1.5 fusion.13
  10.2 0.7 pad_maximum_fusion
  10.9 0.0 all-reduce.3.cloned.1.call-update
  11.0 0.0 copy-start.1
  11.0 0.0 copy-start.7
  11.0 0.0 copy-start.8
  11.0 0.0 reduce-scatter.2.cloned.1.call-start
  12.4 0.7 copy.21
  13.1 3.6 multiply_reduce_fusion
  16.7 1.8 fusion.31
  18.5 0.1 rsqrt.31
  18.7 0.1 copy.26
  18.8 0.1 copy.27
  18.9 0.0 copy-done.1
  18.9 0.0 copy-done.7
  18.9 0.0 copy-done.8
  18.9 4.9 fusion.29
  23.7 0.0 copy-start.4
  23.7 141.3 %all-reduce.3.cloned.1.call-done = bf16[2,4,64,256]{3,2,1,0:T(8,128)(2,1)} async-done(((bf16[2,4,64,256]{3,2,1,0:T(8,128)(2,1)}), bf16[2,4,64,256]{3,2,1,0:T(8,128)(2,1)}) %all-reduce.3.cloned.1.call-update) | async-done | bytes 262160 | tf_op jit(solution)/shard_map/psum | solution.py:29
  165.1 2.0 bitcast_multiply_fusion
  167.0 0.0 copy-done.4
  167.0 0.0 copy-start.3
  167.1 1.7 copy-done.3
  168.7 1.6 slice.43
  170.3 1.9 copy.32
  172.2 0.6 multiply_reduce_fusion.1
  172.9 0.7 multiply_convert_fusion
  173.6 0.8 fusion.7
  174.4 0.0 copy-start.5
  174.4 0.0 copy-start.6
  174.4 2.1 fusion.12
  176.5 1.0 fusion.36
  177.6 0.0 copy-done.5
  177.6 0.0 copy-done.6
  177.6 0.2 fusion.14
  177.8 0.1 copy.24
  178.0 0.1 reshape.75
  178.1 296.8 %all-reduce.4 = bf16[256,128]{1,0:T(8,128)(2,1)S(1)} all-reduce(f32[256,128]{1,0:T(8,128)S(1)} %reshape.75), channel_id=1, replica_groups=mesh['level'=4,'seq'=16,'dp'=4] {'level','seq'}, use_global_device_ids=true, to_apply=%region_4.5 | all-reduce | flops 32768 | bytes 196608 | tf_op jit(solution)/shard_map/psum | solution.py:58
  474.9 0.1 convert_element_type.84
  475.0 4.4 convolution_convert_fusion
  479.4 0.0 reduce-scatter.2.cloned.1.call-update
  479.4 0.0 copy-start.9
  479.5 0.0 copy-start.2
  479.5 7.9 %bitcast_convert_fusion = f32[512,5120]{1,0:T(8,128)} fusion(bf16[1,512,5120]{2,1,0:T(8,128)(2,1)} %param.11), kind=kLoop, calls=%fused_computation.10 | loop fusion | flops 2621440 | bytes 15728640 | tf_op jit(solution)/shard_map/convert_element_type | solution.py:32
  487.4 0.1 dynamic-slice.6
  487.4 0.0 copy-done.9
  487.4 0.1 dynamic-slice_multiply_fusion
  487.5 0.1 convert_element_type.79
  487.6 0.1 copy.33
  487.7 0.9 fusion.39
  488.6 0.0 copy-done.2
  488.6 2.1 fusion.3
  490.7 24.7 %reduce-scatter.2.cloned.1.call-done = bf16[64,1280]{1,0:T(8,128)(2,1)} async-done(((bf16[64,5120]{1,0:T(8,128)(2,1)}), bf16[64,1280]{1,0:T(8,128)(2,1)}) %reduce-scatter.2.cloned.1.call-update) | async-done | bytes 163856 | tf_op jit(solution)/shard_map/reduce_scatter | solution.py:62
  515.4 1.6 fusion.26
  516.9 1.7 fusion.23
  (6 shorter events, 0.1 us)
Async XLA Ops:
  7.2 1.5 copy-start
  7.2 157.9 %all-reduce.3.cloned.1.call-start = ((), (), s32[]{:S(2)}) async-start(), calls=%async_computation.1 | async-start | bytes 524288 | tf_op jit(solution)/shard_map/psum | solution.py:29
  11.0 7.9 %copy-start.1 = (bf16[5120,64]{0,1:T(8,128)(2,1)S(1)}, bf16[5120,64]{0,1:T(8,128)(2,1)}, u32[]{:S(2)}) copy-start(bf16[5120,64]{0,1:T(8,128)(2,1)} %param.13) | copy-start | bytes 1966084
  11.0 7.9 %copy-start.7 = (f32[1,1,512,64]{2,3,1,0:T(8,128)S(1)}, f32[1,1,512,64]{2,3,1,0:T(8,128)}, u32[]{:S(2)}) copy-start(f32[1,1,512,64]{2,3,1,0:T(8,128)} %param.14) | copy-start | bytes 393220
  11.0 7.9 %copy-start.8 = (f32[5120]{0:T(1024)S(1)}, f32[5120]{0:T(1024)}, u32[]{:S(2)}) copy-start(f32[5120]{0:T(1024)} %param.12) | copy-start | bytes 61444
  11.0 504.4 %reduce-scatter.2.cloned.1.call-start = ((), (), s32[]{:S(2)}) async-start(), calls=%async_computation.2 | async-start | bytes 819200 | tf_op jit(solution)/shard_map/reduce_scatter | solution.py:62
  23.7 143.3 %copy-start.4 = (bf16[512,64]{0,1:T(8,128)(2,1)}, bf16[512,64]{0,1:T(8,128)(2,1)S(1)}, u32[]{:S(2)}) copy-start(bf16[512,64]{0,1:T(8,128)(2,1)S(1)} %get-tuple-element.3) | copy-start | bytes 196612
  167.0 1.7 copy-start.3
  174.4 3.2 copy-start.5
  174.4 3.2 copy-start.6
  479.4 8.0 %copy-start.9 = (f32[5120]{0:T(1024)S(1)}, f32[5120]{0:T(1024)}, u32[]{:S(2)}) copy-start(f32[5120]{0:T(1024)} %param.12) | copy-start | bytes 61444
  479.5 9.2 %copy-start.2 = (bf16[5120,64]{0,1:T(8,128)(2,1)S(1)}, bf16[5120,64]{0,1:T(8,128)(2,1)}, u32[]{:S(2)}) copy-start(bf16[5120,64]{0,1:T(8,128)(2,1)} %param.13) | copy-start | bytes 1966084
Sparse Core Ops, SparseCore 0:
  11.2 153.8 all-reduce.2
  479.6 35.7 reduce-scatter.1

commit v2 on v1

v2 whole, which is shorter than its diff:
```python
import functools
import math

import jax
import jax.numpy as jnp
from jax import lax
from jax.experimental import pallas as pl
from jax.experimental.pallas import tpu as pltpu
from jax.sharding import PartitionSpec as P

HD = 128
BF = jnp.bfloat16
F32 = jnp.float32
MESH = pl.DeviceIdType.MESH
NT = (((1,), (1,)), ((), ()))
NN = (((1,), (0,)), ((), ()))
FEAT_CHUNKS = 5
QBLOCK = 256


def mm(a, b, dims=NN):
    return lax.dot_general(a, b, dims, preferred_element_type=F32)


def window(index, part):
    if part % 128 == 0:
        return index * part, part, 0
    assert part % 128 == 64
    offset = lax.rem(index, 2) * 64
    return index * part - offset, part + 64, offset


def kernel(
    sizes,
    sigma_ref, lw_ref, qk_ref, feats_hbm, gain_hbm, gw_hbm, noise_hbm, embed_hbm, pin_hbm, po_hbm, ho_hbm,
    oh_hbm, ow_hbm, og_ref,
    fbuf, gain, gw, noise, ewin, hwin, ewin_s, hwin_s, wbuf,
    wpart, rx, zpart, rz, wfull,
    ssq, x0, rms, xin, qbuf, kbuf, vext, obuf,
    tsend, b1, b2, gfull, psend, crecv, whalf, hout,
    in_sem, feat_sem, out_sem,
    s_rx, r_rx, s_rz, r_rz, s_az, r_az, s_ax, r_ax,
    s_b1, r_b1, s_b2, r_b2, s_b3, r_b3, s_c, r_c, s_k, r_k,
):
    L, S, X = sizes
    D = fbuf.shape[1]
    span = fbuf.shape[0]
    chans = gw.shape[0]
    half = span // 2
    l, s, d = lax.axis_index("level"), lax.axis_index("seq"), lax.axis_index("dp")
    core = lax.rem(s, 2)
    mate = s + 1 - 2 * core

    def remote(src, dst, ssem, rsem, where):
        copy = pltpu.make_async_remote_copy(
            src_ref=src, dst_ref=dst, send_sem=ssem, recv_sem=rsem, device_id=where, device_id_type=MESH
        )
        copy.start()
        return copy

    def drain(ref, sem):
        pltpu.make_async_copy(ref, ref, sem).wait()

    barrier = pltpu.get_barrier_semaphore()
    for o in range(1, X):
        pl.semaphore_signal(barrier, inc=1, device_id={"dp": lax.rem(d + o, X)}, device_id_type=MESH)
    for o in range(1, L):
        pl.semaphore_signal(barrier, inc=1, device_id={"level": lax.rem(l + o, L)}, device_id_type=MESH)
    for o in range(1, S):
        pl.semaphore_signal(barrier, inc=1, device_id={"seq": lax.rem(s + o, S)}, device_id_type=MESH)

    part = pin_hbm.shape[2]
    start_a, win_a, off_a = window(l * X + d, part)
    part_s = D // S
    start_s, win_s, off_s = window(s, part_s)
    if win_a != part:
        start_a = pl.multiple_of(start_a, 128)
        off_a = pl.multiple_of(off_a, 64)
    if win_s != part_s:
        start_s = pl.multiple_of(start_s, 128)
    cols_a, cols_s = pl.ds(start_a, win_a), pl.ds(start_s, win_s)
    inner_rows = pl.ds(off_a, part)

    loads = {}

    def load(name, src, dst):
        k = len(loads)
        copy = pltpu.make_async_copy(src, dst, in_sem.at[k])
        copy.start()
        loads[name] = copy

    load("e", embed_hbm.at[:, :, cols_a], ewin)
    load("p0", pin_hbm.at[0], wbuf.at[0, pl.ds(0, 3), inner_rows])
    load("h", ho_hbm.at[:, :, cols_a], hwin)
    load("o0", po_hbm.at[0], wbuf.at[0, 3, inner_rows])
    load("p1", pin_hbm.at[1], wbuf.at[1, pl.ds(0, 3), inner_rows])
    load("o1", po_hbm.at[1], wbuf.at[1, 3, inner_rows])
    load("gain", gain_hbm, gain)
    load("gw", gw_hbm, gw)
    fc = D // FEAT_CHUNKS
    for c in range(FEAT_CHUNKS):
        pltpu.make_async_copy(
            feats_hbm.at[0, :, pl.ds(c * fc, fc)], fbuf.at[:, pl.ds(c * fc, fc)], feat_sem.at[c]
        ).start()
    load("es", embed_hbm.at[:, :, cols_s], ewin_s)
    load("hs", ho_hbm.at[:, :, cols_s], hwin_s)
    load("noise", noise_hbm, noise)

    if win_a != part:
        pad = pl.ds(pl.multiple_of((part // 64) * 64 - (part // 64) * off_a, 64), 64)
        for n in range(2):
            for j in range(4):
                wbuf[n, j, pad, :] = jnp.zeros((64, wbuf.shape[3]), BF)
    for h in range(2):
        vext[h, :, HD:] = jnp.ones((span, HD), BF)

    def fuse(n):
        for j in range(4):
            left = ewin if j < 3 else hwin
            x = mm(left[n], wbuf[n, j]).astype(BF)
            wpart[n, j, 0:chans, :] = x[:, :HD]
            wpart[n, j, chans : 2 * chans, :] = x[:, HD:]

    def send_rx(n):
        for o in (2, 1, 3) if X == 4 else range(1, X):
            to = lax.rem(d + o, X)
            remote(wpart.at[n, to], rx.at[n, o - 1], s_rx.at[n], r_rx.at[n], {"dp": to})

    def turn_rx(n):
        drain(rx.at[n], r_rx.at[n])
        total = wpart[n, d].astype(F32)
        for o in range(X - 1):
            total = total + rx[n, o].astype(F32)
        zpart[n] = total.astype(BF).reshape(zpart.shape[1:])
        for o in range(L - 1, 0, -1):
            to = lax.rem(l + o, L)
            remote(zpart.at[n, to], rz.at[n, o - 1], s_rz.at[n], r_rz.at[n], {"level": to})

    zrows = 2 * chans // L
    own_z = pl.ds(pl.multiple_of(l * zrows, zrows), zrows)

    def turn_rz(n):
        drain(rz.at[n], r_rz.at[n])
        total = zpart[n, l].astype(F32)
        for o in range(L - 1):
            total = total + rz[n, o].astype(F32)
        wfull[n, d, own_z, :] = total.astype(BF)
        block = wfull.at[n, d, own_z]
        for o in range(L - 1, 0, -1):
            remote(block, block, s_az.at[n], r_az.at[n], {"level": lax.rem(l + o, L)})

    def turn_az(n):
        drain(rz.at[n], r_az.at[n])
        block = wfull.at[n, d]
        for o in (2, 1, 3) if X == 4 else range(1, X):
            remote(block, block, s_ax.at[n], r_ax.at[n], {"dp": lax.rem(d + o, X)})

    def turn_ax(n):
        drain(rx.at[n], r_ax.at[n])

    def feat_chunk(c):
        cols = pl.ds(c * fc, fc)
        pltpu.make_async_copy(feats_hbm.at[0, :, cols], fbuf.at[:, cols], feat_sem.at[c]).wait()
        scaled = (gw[:, c * fc : (c + 1) * fc].astype(F32) * gain[:, c * fc : (c + 1) * fc]).astype(BF)

        def rows_body(i, _):
            rows = pl.ds(pl.multiple_of(i * 64, 64), 64)
            acc = jnp.zeros((64, 128), F32)
            for k in range(fc // 128):
                x = fbuf[rows, c * fc + k * 128 : c * fc + (k + 1) * 128].astype(F32)
                acc = acc + x * x
            ssq[rows, :] = acc if c == 0 else ssq[rows, :] + acc
            return 0

        lax.fori_loop(0, span // 64, rows_body, 0)
        prod = mm(fbuf[:, c * fc : (c + 1) * fc], scaled, NT)
        x0[...] = prod if c == 0 else x0[...] + prod

    loads["e"].wait()
    loads["h"].wait()
    loads["p0"].wait()
    loads["o0"].wait()
    fuse(0)
    pl.semaphore_wait(barrier, X + L + S - 3)
    send_rx(0)
    loads["p1"].wait()
    loads["o1"].wait()
    fuse(1)
    send_rx(1)
    loads["gain"].wait()
    loads["gw"].wait()
    feat_chunk(0)
    turn_rx(0)
    feat_chunk(1)
    turn_rx(1)
    turn_rz(0)
    feat_chunk(2)
    turn_rz(1)
    turn_az(0)
    feat_chunk(3)
    turn_az(1)
    feat_chunk(4)

    loads["noise"].wait()
    loads["es"].wait()
    loads["hs"].wait()
    scale = lax.rsqrt(jnp.sum(ssq[...], axis=-1, keepdims=True) * (1.0 / D) + 1e-06)
    rms[...] = jnp.broadcast_to(scale, rms.shape)
    xz = x0[...] * scale
    x0[...] = xz
    sig = jnp.full((1, chans), sigma_ref[0], F32)
    xin[...] = ((xz + sig * noise[...].T) * lax.rsqrt(sig * sig + 1.0)).astype(BF)

    def straight(n):
        e = ewin_s[n]
        if win_s != part_s:
            lane = lax.broadcasted_iota(jnp.int32, (chans, win_s), 1)
            keep = jnp.logical_and(lane >= off_s, lane < off_s + part_s)
            e = jnp.where(keep, e.astype(F32), 0.0).astype(BF)
        return mm(hwin_s[n], e, NT)

    bent = (straight(1) - straight(0)).astype(BF)
    none = jnp.zeros_like(bent)

    def packed(left, rightT):
        blank = jnp.zeros_like(rightT)
        low = mm(left[:half], jnp.concatenate([rightT, blank], axis=0), NT)
        return low + mm(left[half:], jnp.concatenate([blank, rightT], axis=0), NT)

    total = packed(xin[...], bent)

    fold = math.log2(math.e) / math.sqrt(HD)
    for n in range(2):
        turn_ax(n)
        mats = [jnp.concatenate([wfull[n, j, :chans], wfull[n, j, chans:]], axis=1) for j in range(4)]

        def rows_body(i, _, n=n, mats=mats):
            rows = pl.ds(pl.multiple_of(i * 128, 128), 128)
            x = xin[rows, :]
            for j in range(3):
                a = mm(x, mats[j]) * 0.5
                act = a * jnp.tanh(a) + a
                for h in range(2):
                    t = act[:, h * HD : (h + 1) * HD]
                    if j == 2:
                        vext[h, rows, 0:HD] = t.astype(BF)
                        continue
                    mean = jnp.mean(t * t, axis=-1, keepdims=True)
                    row = qk_ref[2 * n + j : 2 * n + j + 1, :]
                    if j == 0:
                        row = row * fold
                    t = (t * lax.rsqrt(mean + 1e-06) * row).astype(BF)
                    if j == 0:
                        qbuf[h, rows, :] = t
                    else:
                        kbuf[h, rows, :] = t
            return 0

        lax.fori_loop(0, span // 128, rows_body, 0)
        for b in range(span // QBLOCK):
            rows = slice(b * QBLOCK, (b + 1) * QBLOCK)
            for h in range(2):
                weights = jnp.exp2(mm(qbuf[h, rows, :], kbuf[h], NT)).astype(BF)
                both = mm(weights, vext[h])
                obuf[rows, h * HD : (h + 1) * HD] = (both[:, :HD] / both[:, HD:]).astype(BF)
        field = packed(obuf[...], mats[3])
        total = total + field if n else total - field

    tsend[...] = (total * lw_ref[0]).astype(BF)
    trows = half // S

    def chunk(i):
        return pl.ds(pl.multiple_of(i * trows, trows), trows)

    for o in range(1, S):
        to = lax.rem(s + o, S)
        remote(tsend.at[chunk(to)], b1.at[o - 1], s_b1, r_b1, {"seq": to})
    drain(b1, r_b1)
    acc = tsend[chunk(s), :].astype(F32)
    for o in range(S - 1):
        acc = acc + b1[o].astype(F32)
    b2[l] = acc
    for o in range(1, L):
        remote(b2.at[l], b2.at[l], s_b2, r_b2, {"level": lax.rem(l + o, L)})
    drain(b2.at[pl.ds(0, L - 1)], r_b2)
    acc = b2[0]
    for i in range(1, L):
        acc = acc + b2[i]
    gfull[chunk(s), :] = acc.astype(BF)
    for o in range(1, S):
        remote(gfull.at[chunk(s)], gfull.at[chunk(s)], s_b3, r_b3, {"seq": lax.rem(s + o, S)})
    drain(b1, r_b3)

    cut = D // X
    side = cut // 2
    lane = lax.broadcasted_iota(jnp.int32, (half, 2 * chans), 1)
    scaling = jnp.where(lane < chans, rms[0:half, :], rms[half:, :])
    turned = (gfull[...].astype(F32) * scaling).T.astype(BF)
    for o in ((2, 1, 3) if X == 4 else tuple(range(1, X))) + (0,):
        to = lax.rem(d + o, X)
        cols = pl.ds(pl.multiple_of(to * cut + core * side, 128), side)
        term = mm(turned[:chans], fbuf[0:half, cols]) + mm(turned[chans:], fbuf[half:, cols])
        if o:
            psend[o - 1] = term.astype(BF)
            remote(psend.at[o - 1], crecv.at[d], s_c, r_c, {"dp": to})
        else:
            crecv[d] = term.astype(BF)

    rows_h = span // S
    first = s * rows_h
    which = first // half
    own = pl.ds(pl.multiple_of(first, rows_h), rows_h)
    g_own = gfull[pl.ds(pl.multiple_of(first - which * half, rows_h), rows_h), :].astype(F32)
    g_own = jnp.where(which == 0, g_own, pltpu.roll(g_own, chans, 1))[:, :chans]
    inner = jnp.sum(g_own * x0[own, :], axis=-1, keepdims=True) * (1.0 / D)
    scale_own = rms[own, 0:1]
    lessen = scale_own * inner
    g_own = g_own.astype(BF)
    for c in range(FEAT_CHUNKS):
        cols = slice(c * fc, (c + 1) * fc)
        grad = mm(g_own, gw[:, cols]) * gain[:, cols] - fbuf[own, cols].astype(F32) * lessen
        hout[:, cols] = (grad * scale_own).astype(BF)
    send_h = pltpu.make_async_copy(hout, oh_hbm.at[0], out_sem.at[0])
    send_h.start()

    drain(crecv.at[pl.ds(0, X - 1)], r_c)
    acc = crecv[0].astype(F32)
    for i in range(1, X):
        acc = acc + crecv[i].astype(F32)
    factor = 1.0 / math.sqrt(X * span)
    mine = pl.ds(pl.multiple_of(d * cut + core * side, 128), side)
    whalf[core] = acc * (gain[:, mine] * factor)
    remote(whalf.at[core], whalf.at[core], s_k, r_k, {"seq": mate})
    spot = pl.ds(pl.multiple_of(core * side, 128), side)
    send_a = pltpu.make_async_copy(whalf.at[core], ow_hbm.at[:, spot], out_sem.at[1])
    send_a.start()

    drain(psend, s_c)
    for n in range(2):
        drain(rx.at[n], s_rx.at[n])
        drain(rz.at[n], s_rz.at[n])
        drain(rz.at[n], s_az.at[n])
        drain(rx.at[n], s_ax.at[n])
    drain(b1, s_b1)
    drain(b2.at[pl.ds(0, L - 1)], s_b2)
    drain(b1, s_b3)

    drain(whalf.at[0], r_k)
    spot_b = pl.ds(pl.multiple_of((1 - core) * side, 128), side)
    send_b = pltpu.make_async_copy(whalf.at[1 - core], ow_hbm.at[:, spot_b], out_sem.at[2])
    send_b.start()
    for i in range(2):
        cols = pl.ds(pl.multiple_of(d * cut + i * side, 128), side)
        inside = jnp.sum(whalf[i] * gw[:, cols].astype(F32), axis=0, keepdims=True)
        og_ref[:, i * side : (i + 1) * side] = inside / gain[:, cols]
    drain(whalf.at[0], s_k)
    send_h.wait()
    send_a.wait()
    send_b.wait()


def on_device(feats, gen_gain, gen_weight, noise, sigmas, level_weights, embed, proj_in, proj_out, head_out, qk_gain):
    sizes = L, S, X = tuple(lax.axis_size(a) for a in ("level", "seq", "dp"))
    span, D = feats.shape[1:]
    chans = gen_weight.shape[1]
    part = proj_in.shape[2]
    win_a = part if part % 128 == 0 else part + 64
    win_s = D // S if D // S % 128 == 0 else D // S + 64
    half = span // 2
    side = D // X // 2
    rows_h = span // S
    hbm = pl.BlockSpec(memory_space=pl.ANY)
    vmem = pl.BlockSpec(memory_space=pltpu.VMEM)
    smem = pl.BlockSpec(memory_space=pltpu.SMEM)
    V = pltpu.VMEM
    dma = pltpu.SemaphoreType.DMA
    scratch = [
        V((span, D), BF), V((1, D), F32), V((chans, D), BF), V((chans, span), F32),
        V((2, chans, win_a), BF), V((2, chans, win_a), BF), V((2, chans, win_s), BF), V((2, chans, win_s), BF),
        V((2, 4, win_a, 2 * HD), BF),
        V((2, 4, 2 * chans, HD), BF), V((2, X - 1, 2 * chans, HD), BF),
        V((2, L, 2 * chans // L, HD), BF), V((2, L - 1, 2 * chans // L, HD), BF),
        V((2, 4, 2 * chans, HD), BF),
        V((span, 128), F32), V((span, chans), F32), V((span, 128), F32), V((span, chans), BF),
        V((2, span, HD), BF), V((2, span, HD), BF), V((2, span, 2 * HD), BF), V((span, 2 * HD), BF),
        V((half, 2 * chans), BF), V((S - 1, half // S, 2 * chans), BF), V((L, half // S, 2 * chans), F32),
        V((half, 2 * chans), BF), V((X - 1, chans, side), BF), V((X, chans, side), BF), V((2, chans, side), F32),
        V((rows_h, D), BF),
        dma((11,)), dma((FEAT_CHUNKS,)), dma((3,)),
    ] + [dma((2,))] * 8 + [dma] * 10
    out_h, out_w, out_g = pl.pallas_call(
        functools.partial(kernel, sizes),
        out_shape=(
            jax.ShapeDtypeStruct((1, rows_h, D), BF),
            jax.ShapeDtypeStruct((chans, 2 * side), F32),
            jax.ShapeDtypeStruct((1, 2 * side), F32),
        ),
        in_specs=[smem, smem, vmem] + [hbm] * 8,
        out_specs=(hbm, hbm, vmem),
        scratch_shapes=scratch,
        compiler_params=pltpu.CompilerParams(
            collective_id=0, has_side_effects=True, vmem_limit_bytes=56 * 1024 * 1024
        ),
    )(
        sigmas, level_weights, qk_gain.reshape(4, HD), feats, gen_gain[None], gen_weight.T, noise[0, 0].T,
        embed, proj_in, jnp.swapaxes(proj_out, 1, 2), jnp.swapaxes(head_out, 1, 2),
    )
    return out_h, out_w.T, out_g[0]


def solution(mesh):
    in_specs = (
        P("dp", None, None),
        P(),
        P(),
        P("level", "dp", None, None),
        P("level"),
        P("level"),
        P(),
        P(None, None, ("level", "dp"), "seq"),
        P(None, "seq", ("level", "dp")),
        P(),
        P(),
    )
    out_specs = (P("dp", "seq", None), P("dp", None), P("dp"))
    return jax.shard_map(on_device, mesh=mesh, in_specs=in_specs, out_specs=out_specs, check_vma=False)
```

time: 527 us -> 64.8 us (0.12)
  blocking collectives: 297 us -> 0 us
  waiting for transfers between devices: 166 us -> 0 us
  Pallas kernels: 0 us -> 57.9 us
  matrix products: 22.1 us -> 0 us
  other arithmetic: 17.8 us -> 1.31 us
  between operations: 15.7 us -> 1.93 us
    psum x1 -> x0, blocking collectives: 297 us -> none  [on_device(): total = lax.psum(total, ('level', 'seq')).reshape(span, chans)]
    psum x1 -> x0, waiting for transfers between devices: 141 us -> none  [on_device(): fused = lax.psum(fused, ('level', 'dp')).astype(BF)]
    pallas_call x0 -> x1, Pallas kernels: none -> 57.9 us  [on_device(): pl.pallas_call(functools.partial(kernel, sizes), out_shape=(jax.ShapeDtyp...]
    reduce_scatter x1 -> x0, waiting for transfers between devices: 24.7 us -> none  [on_device(): lax.psum_scatter(term.astype(BF), 'dp', scatter_dimension=1, tiled=True)]
    dot_general x11 -> x0, matrix products: 22.1 us -> none  [the longest x1 4.86 us: on_device(): x_zero = jnp.dot(hidden, scaled, preferred_element_type=F32) * rms]
    convert_element_type x3 -> x0, other arithmetic: 8.63 us -> none  [the longest x1 7.9 us: on_device(): wide = hidden.astype(F32)]
    reduce_sum x4 -> x0, other arithmetic: 6.65 us -> none  [the longest x1 3.59 us: on_device(): rms = lax.rsqrt(jnp.mean(wide * wide, axis=-1, keepdims=True) + 1e-06)]
  transfers between devices with their start and end apart: 2 -> 0, of which waited for: 2 -> 0; matrix products, arithmetic and copies ran while one was open for 4% -> 0% of each run, Pallas kernels for 0% -> 0%
where the time goes in v2:
time: 64.8 us; the launch traced here: 64.6 us
  Pallas kernels  57.9 us (89%)
  local copies, waits for them, and re-layouts  3.43 us (5%)
  between operations  1.93 us (3%)
  other arithmetic  1.31 us (2%)
    pallas_call x1, Pallas kernels, on_device(): pl.pallas_call(functools.partial(kernel, sizes), out_shape=(jax.ShapeDtyp...  57.9 us
    unnamed x2, local copies, waits for them, and re-layouts  3.43 us
    pallas_call x1, other arithmetic, on_device(): pl.pallas_call(functools.partial(kernel, sizes), out_shape=(jax.ShapeDtyp...  1.31 us

profile of v2, /device:TPU:1, one launch (start us, length us, event | category | flops | bytes accessed | tf_op | source)
XLA Modules:
  0.0 64.6 jit_solution(2322064157634673848)
XLA Ops:
  1.9 57.9 %shard_map.130 = (bf16[1,32,5120]{2,1,0:T(8,128)(2,1)}, f32[64,1280]{1,0:T(8,128)}, f32[1,1280]{1,0:T(1,128)}) custom-call(f32[1]{0:T(128)S(6)} %copy.16.sigma_ref, f32[1]{0:T(128)S(6)} %copy.17.lw_ref, f32[4,128]{1,0:T(4,128)} %bitcast.15, bf16[1,512,5120]{2,1,0:T(8,128)(2,1)} %feats_hbm.1, f32[1,5120]{1,0:T(1,128)} %bitcast.14, bf16[64,5120]{1,0:T(8,128)(2,1)} %bitcast.10, ...), custom_call_target="tpu_custom_call" | custom-call | tf_op jit(solution)/shard_map/pallas_call | solution.py:391
  59.8 1.3 %reduce = f32[1280]{0:T(1024)} reduce(f32[1,1280]{1,0:T(1,128)} %get-tuple-element.8, f32[]{:T(128)} %constant.4), dimensions={0}, to_apply=%get-tuple-element.8.reduce_sub_computation | reduce | bytes 10244 | tf_op jit(solution)/shard_map/pallas_call | solution.py:391
  61.1 1.7 %copy.18 = bf16[1,32,5120]{2,1,0:T(8,128)(2,1)} copy(bf16[1,32,5120]{2,1,0:T(8,128)(2,1)} %get-tuple-element.12) | data formatting | bytes 655360
  62.9 1.7 %copy.19 = f32[1280,64]{0,1:T(8,128)} copy(f32[1280,64]{0,1:T(8,128)} %bitcast.12) | data formatting | bytes 655360

commit v3 on v2

--- a/solution.py
+++ b/solution.py
@@ -35,11 +35,11 @@
     sigma_ref, lw_ref, qk_ref, feats_hbm, gain_hbm, gw_hbm, noise_hbm, embed_hbm, pin_hbm, po_hbm, ho_hbm,
     oh_hbm, ow_hbm, og_ref,
     fbuf, gain, gw, noise, ewin, hwin, ewin_s, hwin_s, wbuf,
-    wpart, rx, zpart, rz, wfull,
+    wpart, rx, wfull,
     ssq, x0, rms, xin, qbuf, kbuf, vext, obuf,
     tsend, b1, b2, gfull, psend, crecv, whalf, hout,
     in_sem, feat_sem, out_sem,
-    s_rx, r_rx, s_rz, r_rz, s_az, r_az, s_ax, r_ax,
+    s_rx, r_rx, s_ax, r_ax,
     s_b1, r_b1, s_b2, r_b2, s_b3, r_b3, s_c, r_c, s_k, r_k,
 ):
     L, S, X = sizes
@@ -51,6 +51,15 @@
     core = lax.rem(s, 2)
     mate = s + 1 - 2 * core
 
+    team = [
+        {"level": lax.rem(l + a, L), "dp": lax.rem(d + b, X)} for a in range(L) for b in range(X) if a or b
+    ]
+    pairs = S // 2
+    chips = L * pairs
+
+    def chip(i):
+        return {"level": lax.rem(l + i % L, L), "seq": 2 * lax.rem(s // 2 + i // L, pairs) + core}
+
     def remote(src, dst, ssem, rsem, where):
         copy = pltpu.make_async_remote_copy(
             src_ref=src, dst_ref=dst, send_sem=ssem, recv_sem=rsem, device_id=where, device_id_type=MESH
@@ -62,12 +71,8 @@
         pltpu.make_async_copy(ref, ref, sem).wait()
 
     barrier = pltpu.get_barrier_semaphore()
-    for o in range(1, X):
-        pl.semaphore_signal(barrier, inc=1, device_id={"dp": lax.rem(d + o, X)}, device_id_type=MESH)
-    for o in range(1, L):
-        pl.semaphore_signal(barrier, inc=1, device_id={"level": lax.rem(l + o, L)}, device_id_type=MESH)
-    for o in range(1, S):
-        pl.semaphore_signal(barrier, inc=1, device_id={"seq": lax.rem(s + o, S)}, device_id_type=MESH)
+    for peer in team + [chip(i) for i in range(1, chips)] + [{"seq": mate}]:
+        pl.semaphore_signal(barrier, inc=1, device_id=peer, device_id_type=MESH)
 
     part = pin_hbm.shape[2]
     start_a, win_a, off_a = window(l * X + d, part)
@@ -118,45 +123,29 @@
         for j in range(4):
             left = ewin if j < 3 else hwin
             x = mm(left[n], wbuf[n, j]).astype(BF)
-            wpart[n, j, 0:chans, :] = x[:, :HD]
-            wpart[n, j, chans : 2 * chans, :] = x[:, HD:]
-
-    def send_rx(n):
-        for o in (2, 1, 3) if X == 4 else range(1, X):
-            to = lax.rem(d + o, X)
-            remote(wpart.at[n, to], rx.at[n, o - 1], s_rx.at[n], r_rx.at[n], {"dp": to})
-
-    def turn_rx(n):
+            base = 2 * j * chans
+            wpart[n, base : base + chans, :] = x[:, :HD]
+            wpart[n, base + chans : base + 2 * chans, :] = x[:, HD:]
+
+    share = 8 * chans // (L * X)
+
+    def share_rows(peer):
+        return pl.ds(pl.multiple_of((peer["level"] * X + peer["dp"]) * share, share), share)
+
+    own_share = share_rows({"level": l, "dp": d})
+
+    def send_shares(n):
+        for o, peer in enumerate(team):
+            remote(wpart.at[n, share_rows(peer)], rx.at[n, o], s_rx.at[n], r_rx.at[n], peer)
+
+    def sum_shares(n):
         drain(rx.at[n], r_rx.at[n])
-        total = wpart[n, d].astype(F32)
-        for o in range(X - 1):
+        total = wpart[n, own_share, :].astype(F32)
+        for o in range(len(team)):
             total = total + rx[n, o].astype(F32)
-        zpart[n] = total.astype(BF).reshape(zpart.shape[1:])
-        for o in range(L - 1, 0, -1):
-            to = lax.rem(l + o, L)
-            remote(zpart.at[n, to], rz.at[n, o - 1], s_rz.at[n], r_rz.at[n], {"level": to})
-
-    zrows = 2 * chans // L
-    own_z = pl.ds(pl.multiple_of(l * zrows, zrows), zrows)
-
-    def turn_rz(n):
-        drain(rz.at[n], r_rz.at[n])
-        total = zpart[n, l].astype(F32)
-        for o in range(L - 1):
-            total = total + rz[n, o].astype(F32)
-        wfull[n, d, own_z, :] = total.astype(BF)
-        block = wfull.at[n, d, own_z]
-        for o in range(L - 1, 0, -1):
-            remote(block, block, s_az.at[n], r_az.at[n], {"level": lax.rem(l + o, L)})
-
-    def turn_az(n):
-        drain(rz.at[n], r_az.at[n])
-        block = wfull.at[n, d]
-        for o in (2, 1, 3) if X == 4 else range(1, X):
-            remote(block, block, s_ax.at[n], r_ax.at[n], {"dp": lax.rem(d + o, X)})
-
-    def turn_ax(n):
-        drain(rx.at[n], r_ax.at[n])
+        wfull[n, own_share, :] = total.astype(BF)
+        for peer in team:
+            remote(wfull.at[n, own_share], wfull.at[n, own_share], s_ax.at[n], r_ax.at[n], peer)
 
     def feat_chunk(c):
         cols = pl.ds(c * fc, fc)
@@ -181,25 +170,18 @@
     loads["p0"].wait()
     loads["o0"].wait()
     fuse(0)
-    pl.semaphore_wait(barrier, X + L + S - 3)
-    send_rx(0)
     loads["p1"].wait()
     loads["o1"].wait()
     fuse(1)
-    send_rx(1)
     loads["gain"].wait()
     loads["gw"].wait()
     feat_chunk(0)
-    turn_rx(0)
     feat_chunk(1)
-    turn_rx(1)
-    turn_rz(0)
-    feat_chunk(2)
-    turn_rz(1)
-    turn_az(0)
-    feat_chunk(3)
-    turn_az(1)
-    feat_chunk(4)
+    pl.semaphore_wait(barrier, L * X + chips - 1)
+    send_shares(0)
+    send_shares(1)
+    for c in range(2, FEAT_CHUNKS):
+        feat_chunk(c)
 
     loads["noise"].wait()
     loads["es"].wait()
@@ -227,12 +209,17 @@
         low = mm(left[:half], jnp.concatenate([rightT, blank], axis=0), NT)
         return low + mm(left[half:], jnp.concatenate([blank, rightT], axis=0), NT)
 
+    sum_shares(0)
+    sum_shares(1)
     total = packed(xin[...], bent)
 
     fold = math.log2(math.e) / math.sqrt(HD)
     for n in range(2):
-        turn_ax(n)
-        mats = [jnp.concatenate([wfull[n, j, :chans], wfull[n, j, chans:]], axis=1) for j in range(4)]
+        drain(rx.at[n], r_ax.at[n])
+        mats = [
+            jnp.concatenate([wfull[n, (2 * j + h) * chans : (2 * j + h + 1) * chans] for h in range(2)], axis=1)
+            for j in range(4)
+        ]
 
         def rows_body(i, _, n=n, mats=mats):
             rows = pl.ds(pl.multiple_of(i * 128, 128), 128)
@@ -267,29 +254,33 @@
         total = total + field if n else total - field
 
     tsend[...] = (total * lw_ref[0]).astype(BF)
-    trows = half // S
-
-    def chunk(i):
-        return pl.ds(pl.multiple_of(i * trows, trows), trows)
-
-    for o in range(1, S):
-        to = lax.rem(s + o, S)
-        remote(tsend.at[chunk(to)], b1.at[o - 1], s_b1, r_b1, {"seq": to})
-    drain(b1, r_b1)
-    acc = tsend[chunk(s), :].astype(F32)
-    for o in range(S - 1):
-        acc = acc + b1[o].astype(F32)
-    b2[l] = acc
-    for o in range(1, L):
-        remote(b2.at[l], b2.at[l], s_b2, r_b2, {"level": lax.rem(l + o, L)})
-    drain(b2.at[pl.ds(0, L - 1)], r_b2)
-    acc = b2[0]
-    for i in range(1, L):
-        acc = acc + b2[i]
-    gfull[chunk(s), :] = acc.astype(BF)
-    for o in range(1, S):
-        remote(gfull.at[chunk(s)], gfull.at[chunk(s)], s_b3, r_b3, {"seq": lax.rem(s + o, S)})
-    drain(b1, r_b3)
+    blocks = L * pairs // 2
+    trows = half // blocks
+
+    def block_of(peer):
+        return pl.ds(pl.multiple_of((peer["seq"] // 4 * L + peer["level"]) * trows, trows), trows)
+
+    me = {"level": l, "seq": s}
+    spot_b = s // 2 * L + l
+    b1[spot_b] = tsend[block_of(me), :]
+    for i in range(1, chips):
+        peer = chip(i)
+        remote(tsend.at[block_of(peer)], b1.at[spot_b], s_b1, r_b1, peer)
+    drain(b1.at[pl.ds(0, chips - 1)], r_b1)
+    acc = b1[0].astype(F32)
+    for i in range(1, chips):
+        acc = acc + b1[i].astype(F32)
+    b2[core] = acc
+    remote(b2.at[core], b2.at[core], s_b2, r_b2, {"seq": mate})
+    drain(b2.at[0], r_b2)
+    mine_b = block_of(me)
+    gfull[mine_b, :] = (b2[0] + b2[1]).astype(BF)
+    near = [
+        {"level": lax.rem(l + i % L, L), "seq": lax.rem(s + 4 * (i // L), S)} for i in range(1, blocks)
+    ]
+    for peer in near:
+        remote(gfull.at[mine_b], gfull.at[mine_b], s_b3, r_b3, peer)
+    drain(b1.at[pl.ds(0, blocks - 1)], r_b3)
 
     cut = D // X
     side = cut // 2
@@ -338,16 +329,14 @@
     drain(psend, s_c)
     for n in range(2):
         drain(rx.at[n], s_rx.at[n])
-        drain(rz.at[n], s_rz.at[n])
-        drain(rz.at[n], s_az.at[n])
         drain(rx.at[n], s_ax.at[n])
-    drain(b1, s_b1)
-    drain(b2.at[pl.ds(0, L - 1)], s_b2)
-    drain(b1, s_b3)
+    drain(b1.at[pl.ds(0, chips - 1)], s_b1)
+    drain(b2.at[0], s_b2)
+    drain(b1.at[pl.ds(0, blocks - 1)], s_b3)
 
     drain(whalf.at[0], r_k)
-    spot_b = pl.ds(pl.multiple_of((1 - core) * side, 128), side)
-    send_b = pltpu.make_async_copy(whalf.at[1 - core], ow_hbm.at[:, spot_b], out_sem.at[2])
+    spot_o = pl.ds(pl.multiple_of((1 - core) * side, 128), side)
+    send_b = pltpu.make_async_copy(whalf.at[1 - core], ow_hbm.at[:, spot_o], out_sem.at[2])
     send_b.start()
     for i in range(2):
         cols = pl.ds(pl.multiple_of(d * cut + i * side, 128), side)
@@ -378,16 +367,15 @@
         V((span, D), BF), V((1, D), F32), V((chans, D), BF), V((chans, span), F32),
         V((2, chans, win_a), BF), V((2, chans, win_a), BF), V((2, chans, win_s), BF), V((2, chans, win_s), BF),
         V((2, 4, win_a, 2 * HD), BF),
-        V((2, 4, 2 * chans, HD), BF), V((2, X - 1, 2 * chans, HD), BF),
-        V((2, L, 2 * chans // L, HD), BF), V((2, L - 1, 2 * chans // L, HD), BF),
-        V((2, 4, 2 * chans, HD), BF),
+        V((2, 8 * chans, HD), BF), V((2, L * X - 1, 8 * chans // (L * X), HD), BF), V((2, 8 * chans, HD), BF),
         V((span, 128), F32), V((span, chans), F32), V((span, 128), F32), V((span, chans), BF),
         V((2, span, HD), BF), V((2, span, HD), BF), V((2, span, 2 * HD), BF), V((span, 2 * HD), BF),
-        V((half, 2 * chans), BF), V((S - 1, half // S, 2 * chans), BF), V((L, half // S, 2 * chans), F32),
+        V((half, 2 * chans), BF), V((L * S // 2, 4 * half // (L * S), 2 * chans), BF),
+        V((2, 4 * half // (L * S), 2 * chans), F32),
         V((half, 2 * chans), BF), V((X - 1, chans, side), BF), V((X, chans, side), BF), V((2, chans, side), F32),
         V((rows_h, D), BF),
         dma((11,)), dma((FEAT_CHUNKS,)), dma((3,)),
-    ] + [dma((2,))] * 8 + [dma] * 10
+    ] + [dma((2,))] * 4 + [dma] * 10
     out_h, out_w, out_g = pl.pallas_call(
         functools.partial(kernel, sizes),
         out_shape=(

time: 64.8 us -> 59 us (0.910)
  Pallas kernels: 57.9 us -> 52.1 us
    pallas_call x1, Pallas kernels: 57.9 us -> 52.1 us  [on_device(): pl.pallas_call(functools.partial(kernel, sizes), out_shape=(jax.ShapeDtyp...]
where the time goes in v3:
time: 59 us; the launch traced here: 58.8 us
  Pallas kernels  52.1 us (88%)
  local copies, waits for them, and re-layouts  3.43 us (6%)
  between operations  1.93 us (3%)
  other arithmetic  1.31 us (2%)
    pallas_call x1, Pallas kernels, on_device(): pl.pallas_call(functools.partial(kernel, sizes), out_shape=(jax.ShapeDtyp...  52.1 us
    unnamed x2, local copies, waits for them, and re-layouts  3.43 us
    pallas_call x1, other arithmetic, on_device(): pl.pallas_call(functools.partial(kernel, sizes), out_shape=(jax.ShapeDtyp...  1.31 us

profile of v3, /device:TPU:1, one launch (start us, length us, event | category | flops | bytes accessed | tf_op | source)
XLA Modules:
  0.0 58.8 jit_solution(11093311050432361940)
XLA Ops:
  1.9 52.1 %shard_map.130 = (bf16[1,32,5120]{2,1,0:T(8,128)(2,1)}, f32[64,1280]{1,0:T(8,128)}, f32[1,1280]{1,0:T(1,128)}) custom-call(f32[1]{0:T(128)S(6)} %copy.16.sigma_ref, f32[1]{0:T(128)S(6)} %copy.17.lw_ref, f32[4,128]{1,0:T(4,128)} %bitcast.15, bf16[1,512,5120]{2,1,0:T(8,128)(2,1)} %feats_hbm.1, f32[1,5120]{1,0:T(1,128)} %bitcast.14, bf16[64,5120]{1,0:T(8,128)(2,1)} %bitcast.10, ...), custom_call_target="tpu_custom_call" | custom-call | tf_op jit(solution)/shard_map/pallas_call | solution.py:379
  54.0 1.3 %reduce = f32[1280]{0:T(1024)} reduce(f32[1,1280]{1,0:T(1,128)} %get-tuple-element.8, f32[]{:T(128)} %constant.4), dimensions={0}, to_apply=%get-tuple-element.8.reduce_sub_computation | reduce | bytes 10244 | tf_op jit(solution)/shard_map/pallas_call | solution.py:379
  55.3 1.7 %copy.18 = bf16[1,32,5120]{2,1,0:T(8,128)(2,1)} copy(bf16[1,32,5120]{2,1,0:T(8,128)(2,1)} %get-tuple-element.12) | data formatting | bytes 655360
  57.1 1.7 %copy.19 = f32[1280,64]{0,1:T(8,128)} copy(f32[1280,64]{0,1:T(8,128)} %bitcast.12) | data formatting | bytes 655360

commit v4 on v3

--- a/solution.py
+++ b/solution.py
@@ -32,13 +32,13 @@
 
 def kernel(
     sizes,
-    sigma_ref, lw_ref, qk_ref, feats_hbm, gain_hbm, gw_hbm, noise_hbm, embed_hbm, pin_hbm, po_hbm, ho_hbm,
-    oh_hbm, ow_hbm, og_ref,
-    fbuf, gain, gw, noise, ewin, hwin, ewin_s, hwin_s, wbuf,
+    sigma_ref, lw_ref, qk_hbm, feats_hbm, gain_hbm, gw_hbm, noise_hbm, embed_hbm, pin_hbm, po_hbm, ho_hbm,
+    oh_ref, ow_ref, og_ref,
+    qk_ref, fbuf, gain, gw, noise, ewin, hwin, ewin_s, hwin_s, wbuf,
     wpart, rx, wfull,
     ssq, x0, rms, xin, qbuf, kbuf, vext, obuf,
-    tsend, b1, b2, gfull, psend, crecv, whalf, hout,
-    in_sem, feat_sem, out_sem,
+    tsend, b1, b2, gfull, psend, crecv,
+    in_sem, feat_sem,
     s_rx, r_rx, s_ax, r_ax,
     s_b1, r_b1, s_b2, r_b2, s_b3, r_b3, s_c, r_c, s_k, r_k,
 ):
@@ -110,6 +110,7 @@
     load("es", embed_hbm.at[:, :, cols_s], ewin_s)
     load("hs", ho_hbm.at[:, :, cols_s], hwin_s)
     load("noise", noise_hbm, noise)
+    load("qk", qk_hbm, qk_ref)
 
     if win_a != part:
         pad = pl.ds(pl.multiple_of((part // 64) * 64 - (part // 64) * off_a, 64), 64)
@@ -186,6 +187,7 @@
     loads["noise"].wait()
     loads["es"].wait()
     loads["hs"].wait()
+    loads["qk"].wait()
     scale = lax.rsqrt(jnp.sum(ssq[...], axis=-1, keepdims=True) * (1.0 / D) + 1e-06)
     rms[...] = jnp.broadcast_to(scale, rms.shape)
     xz = x0[...] * scale
@@ -310,9 +312,7 @@
     for c in range(FEAT_CHUNKS):
         cols = slice(c * fc, (c + 1) * fc)
         grad = mm(g_own, gw[:, cols]) * gain[:, cols] - fbuf[own, cols].astype(F32) * lessen
-        hout[:, cols] = (grad * scale_own).astype(BF)
-    send_h = pltpu.make_async_copy(hout, oh_hbm.at[0], out_sem.at[0])
-    send_h.start()
+        oh_ref[:, cols] = (grad * scale_own).astype(BF)
 
     drain(crecv.at[pl.ds(0, X - 1)], r_c)
     acc = crecv[0].astype(F32)
@@ -320,12 +320,9 @@
         acc = acc + crecv[i].astype(F32)
     factor = 1.0 / math.sqrt(X * span)
     mine = pl.ds(pl.multiple_of(d * cut + core * side, 128), side)
-    whalf[core] = acc * (gain[:, mine] * factor)
-    remote(whalf.at[core], whalf.at[core], s_k, r_k, {"seq": mate})
     spot = pl.ds(pl.multiple_of(core * side, 128), side)
-    send_a = pltpu.make_async_copy(whalf.at[core], ow_hbm.at[:, spot], out_sem.at[1])
-    send_a.start()
-
+    ow_ref[:, spot] = acc * (gain[:, mine] * factor)
+    remote(ow_ref.at[:, spot], ow_ref.at[:, spot], s_k, r_k, {"seq": mate})
     drain(psend, s_c)
     for n in range(2):
         drain(rx.at[n], s_rx.at[n])
@@ -334,18 +331,11 @@
     drain(b2.at[0], s_b2)
     drain(b1.at[pl.ds(0, blocks - 1)], s_b3)
 
-    drain(whalf.at[0], r_k)
-    spot_o = pl.ds(pl.multiple_of((1 - core) * side, 128), side)
-    send_b = pltpu.make_async_copy(whalf.at[1 - core], ow_hbm.at[:, spot_o], out_sem.at[2])
-    send_b.start()
-    for i in range(2):
-        cols = pl.ds(pl.multiple_of(d * cut + i * side, 128), side)
-        inside = jnp.sum(whalf[i] * gw[:, cols].astype(F32), axis=0, keepdims=True)
-        og_ref[:, i * side : (i + 1) * side] = inside / gain[:, cols]
-    drain(whalf.at[0], s_k)
-    send_h.wait()
-    send_a.wait()
-    send_b.wait()
+    drain(ow_ref.at[:, 0:side], r_k)
+    block = pl.ds(pl.multiple_of(d * cut, 128), cut)
+    inside = jnp.sum(ow_ref[...] * gw[:, block].astype(F32), axis=0, keepdims=True)
+    og_ref[...] = inside / gain[:, block]
+    drain(ow_ref.at[:, 0:side], s_k)
 
 
 def on_device(feats, gen_gain, gen_weight, noise, sigmas, level_weights, embed, proj_in, proj_out, head_out, qk_gain):
@@ -358,12 +348,13 @@
     half = span // 2
     side = D // X // 2
     rows_h = span // S
-    hbm = pl.BlockSpec(memory_space=pl.ANY)
+    hbm = pl.BlockSpec(memory_space=pltpu.HBM)
     vmem = pl.BlockSpec(memory_space=pltpu.VMEM)
     smem = pl.BlockSpec(memory_space=pltpu.SMEM)
     V = pltpu.VMEM
     dma = pltpu.SemaphoreType.DMA
     scratch = [
+        V((4, HD), F32),
         V((span, D), BF), V((1, D), F32), V((chans, D), BF), V((chans, span), F32),
         V((2, chans, win_a), BF), V((2, chans, win_a), BF), V((2, chans, win_s), BF), V((2, chans, win_s), BF),
         V((2, 4, win_a, 2 * HD), BF),
@@ -372,28 +363,34 @@
         V((2, span, HD), BF), V((2, span, HD), BF), V((2, span, 2 * HD), BF), V((span, 2 * HD), BF),
         V((half, 2 * chans), BF), V((L * S // 2, 4 * half // (L * S), 2 * chans), BF),
         V((2, 4 * half // (L * S), 2 * chans), F32),
-        V((half, 2 * chans), BF), V((X - 1, chans, side), BF), V((X, chans, side), BF), V((2, chans, side), F32),
-        V((rows_h, D), BF),
-        dma((11,)), dma((FEAT_CHUNKS,)), dma((3,)),
+        V((half, 2 * chans), BF), V((X - 1, chans, side), BF), V((X, chans, side), BF),
+        dma((12,)), dma((FEAT_CHUNKS,)),
     ] + [dma((2,))] * 4 + [dma] * 10
     out_h, out_w, out_g = pl.pallas_call(
         functools.partial(kernel, sizes),
         out_shape=(
-            jax.ShapeDtypeStruct((1, rows_h, D), BF),
-            jax.ShapeDtypeStruct((chans, 2 * side), F32),
-            jax.ShapeDtypeStruct((1, 2 * side), F32),
+            V((rows_h, D), BF),
+            V((chans, 2 * side), F32),
+            V((1, 2 * side), F32),
         ),
-        in_specs=[smem, smem, vmem] + [hbm] * 8,
-        out_specs=(hbm, hbm, vmem),
+        in_specs=[smem] * 2 + [hbm] * 9,
+        out_specs=(vmem, vmem, vmem),
         scratch_shapes=scratch,
         compiler_params=pltpu.CompilerParams(
-            collective_id=0, has_side_effects=True, vmem_limit_bytes=56 * 1024 * 1024
+            collective_id=0, has_side_effects=True, vmem_limit_bytes=40 * 1024 * 1024
         ),
     )(
-        sigmas, level_weights, qk_gain.reshape(4, HD), feats, gen_gain[None], gen_weight.T, noise[0, 0].T,
-        embed, proj_in, jnp.swapaxes(proj_out, 1, 2), jnp.swapaxes(head_out, 1, 2),
+        sigmas,
+        level_weights,
+        *(
+            pltpu.with_memory_space_constraint(a, pltpu.HBM)
+            for a in (
+                qk_gain.reshape(4, HD), feats, gen_gain[None], gen_weight.T, noise[0, 0].T,
+                embed, proj_in, jnp.swapaxes(proj_out, 1, 2), jnp.swapaxes(head_out, 1, 2),
+            )
+        ),
     )
-    return out_h, out_w.T, out_g[0]
+    return out_h[None], out_w.T, out_g[0]
 
 
 def solution(mesh):

time: 59 us -> 54.5 us (0.924)
  local copies, waits for them, and re-layouts: 3.43 us -> 1.45 us
  Pallas kernels: 52.1 us -> 50.4 us
  other arithmetic: 1.31 us -> 0.62 us
    unnamed x2, local copies, waits for them, and re-layouts: 3.43 us -> 1.45 us
    pallas_call x1, Pallas kernels: 52.1 us -> 50.4 us  [on_device(): pl.pallas_call(functools.partial(kernel, sizes), out_shape=(V((rows_h, D)...]
    pallas_call x1, other arithmetic: 1.31 us -> 0.62 us  [on_device(): pl.pallas_call(functools.partial(kernel, sizes), out_shape=(V((rows_h, D)...]
where the time goes in v4:
time: 54.5 us; the launch traced here: 54.4 us
  Pallas kernels  50.4 us (92%)
  between operations  1.93 us (4%)
  local copies, waits for them, and re-layouts  1.45 us (3%)
  other arithmetic  0.62 us (1%)
    pallas_call x1, Pallas kernels, on_device(): pl.pallas_call(functools.partial(kernel, sizes), out_shape=(V((rows_h, D)...  50.4 us
    unnamed x2, local copies, waits for them, and re-layouts  1.45 us

profile of v4, /device:TPU:1, one launch (start us, length us, event | category | flops | bytes accessed | tf_op | source)
XLA Modules:
  0.0 54.4 jit_solution(977877999279037084)
XLA Ops:
  1.9 50.4 %shard_map.130 = (bf16[32,5120]{1,0:T(8,128)(2,1)S(1)}, f32[64,1280]{1,0:T(8,128)S(1)}, f32[1,1280]{1,0:T(1,128)S(1)}) custom-call(f32[1]{0:T(128)S(6)} %copy.18.sigma_ref, f32[1]{0:T(128)S(6)} %copy.19.lw_ref, f32[4,128]{1,0:T(4,128)} %bitcast.17, bf16[1,512,5120]{2,1,0:T(8,128)(2,1)} %feats_hbm.1, f32[1,5120]{1,0:T(1,128)} %bitcast.16, ...), custom_call_target="tpu_custom_call" | custom-call | tf_op jit(solution)/shard_map/pallas_call | solution.py:369
  52.3 0.7 %copy.16 = bf16[1,32,5120]{2,1,0:T(8,128)(2,1)} copy(bf16[1,32,5120]{2,1,0:T(8,128)(2,1)S(1)} %bitcast.11) | data formatting | bytes 655360
  53.1 0.7 %copy.17 = f32[1280,64]{0,1:T(8,128)} copy(f32[1280,64]{0,1:T(8,128)S(1)} %bitcast.10) | data formatting | bytes 655360
  53.8 0.6 %reduce = f32[1280]{0:T(1024)} reduce(f32[1,1280]{1,0:T(1,128)S(1)} %get-tuple-element.8, f32[]{:T(128)} %constant.4), dimensions={0}, to_apply=%get-tuple-element.8.reduce_sub_computation | reduce | bytes 10244 | tf_op jit(solution)/shard_map/pallas_call | solution.py:369

commit v5 on v4

--- a/solution.py
+++ b/solution.py
@@ -51,14 +51,24 @@
     core = lax.rem(s, 2)
     mate = s + 1 - 2 * core
 
+    mirror = [l, l + 1 - 2 * lax.rem(l, 2), l + 2 - 4 * (l // 2), L - 1 - l]
     team = [
-        {"level": lax.rem(l + a, L), "dp": lax.rem(d + b, X)} for a in range(L) for b in range(X) if a or b
+        {"level": mirror[a], "dp": lax.rem(d + b, X)} for a in (3, 2, 1, 0) for b in (2, 1, 3, 0) if a or b
     ]
-    pairs = S // 2
-    chips = L * pairs
-
-    def chip(i):
-        return {"level": lax.rem(l + i % L, L), "seq": 2 * lax.rem(s // 2 + i // L, pairs) + core}
+    Z, Y = 2 * L, S // 4
+    chips = Z * Y
+    y, z = s // 4, lax.rem(s // 2, 2) * L + l
+
+    def chip(step_y, step_z):
+        to_y, to_z = lax.rem(y + step_y, Y), lax.rem(z + step_z, Z)
+        return {"level": lax.rem(to_z, L), "seq": 4 * to_y + 2 * (to_z // L) + core}
+
+    def around(steps_z):
+        steps = [(a, b) for a in range(Y) for b in steps_z if a or b]
+        far = lambda step: min(step[0], Y - step[0]) + min(step[1], Z - step[1])
+        return [chip(*step) for step in sorted(steps, key=far, reverse=True)]
+
+    others = around(range(Z))
 
     def remote(src, dst, ssem, rsem, where):
         copy = pltpu.make_async_remote_copy(
@@ -71,7 +81,7 @@
         pltpu.make_async_copy(ref, ref, sem).wait()
 
     barrier = pltpu.get_barrier_semaphore()
-    for peer in team + [chip(i) for i in range(1, chips)] + [{"seq": mate}]:
+    for peer in others + team + [{"seq": mate}]:
         pl.semaphore_signal(barrier, inc=1, device_id=peer, device_id_type=MESH)
 
     part = pin_hbm.shape[2]
@@ -245,7 +255,7 @@
                         kbuf[h, rows, :] = t
             return 0
 
-        lax.fori_loop(0, span // 128, rows_body, 0)
+        lax.fori_loop(0, span // 128, rows_body, 0, unroll=True)
         for b in range(span // QBLOCK):
             rows = slice(b * QBLOCK, (b + 1) * QBLOCK)
             for h in range(2):
@@ -256,7 +266,7 @@
         total = total + field if n else total - field
 
     tsend[...] = (total * lw_ref[0]).astype(BF)
-    blocks = L * pairs // 2
+    blocks = chips // 2
     trows = half // blocks
 
     def block_of(peer):
@@ -265,8 +275,7 @@
     me = {"level": l, "seq": s}
     spot_b = s // 2 * L + l
     b1[spot_b] = tsend[block_of(me), :]
-    for i in range(1, chips):
-        peer = chip(i)
+    for peer in others:
         remote(tsend.at[block_of(peer)], b1.at[spot_b], s_b1, r_b1, peer)
     drain(b1.at[pl.ds(0, chips - 1)], r_b1)
     acc = b1[0].astype(F32)
@@ -277,10 +286,7 @@
     drain(b2.at[0], r_b2)
     mine_b = block_of(me)
     gfull[mine_b, :] = (b2[0] + b2[1]).astype(BF)
-    near = [
-        {"level": lax.rem(l + i % L, L), "seq": lax.rem(s + 4 * (i // L), S)} for i in range(1, blocks)
-    ]
-    for peer in near:
+    for peer in around((0, 1, 2, Z - 1)):
         remote(gfull.at[mine_b], gfull.at[mine_b], s_b3, r_b3, peer)
     drain(b1.at[pl.ds(0, blocks - 1)], r_b3)
 

time: 54.5 us -> 51.3 us (0.941)
  Pallas kernels: 50.4 us -> 47.2 us
    pallas_call x1, Pallas kernels: 50.4 us -> 47.2 us  [on_device(): pl.pallas_call(functools.partial(kernel, sizes), out_shape=(V((rows_h, D)...]
where the time goes in v5:
time: 51.3 us; the launch traced here: 51.2 us
  Pallas kernels  47.2 us (92%)
  between operations  1.93 us (4%)
  local copies, waits for them, and re-layouts  1.45 us (3%)
  other arithmetic  0.62 us (1%)
    pallas_call x1, Pallas kernels, on_device(): pl.pallas_call(functools.partial(kernel, sizes), out_shape=(V((rows_h, D)...  47.2 us
    unnamed x2, local copies, waits for them, and re-layouts  1.45 us

profile of v5, /device:TPU:1, one launch (start us, length us, event | category | flops | bytes accessed | tf_op | source)
XLA Modules:
  0.0 51.2 jit_solution(13891133966870030803)
XLA Ops:
  1.9 47.2 %shard_map.130 = (bf16[32,5120]{1,0:T(8,128)(2,1)S(1)}, f32[64,1280]{1,0:T(8,128)S(1)}, f32[1,1280]{1,0:T(1,128)S(1)}) custom-call(f32[1]{0:T(128)S(6)} %copy.18.sigma_ref, f32[1]{0:T(128)S(6)} %copy.19.lw_ref, f32[4,128]{1,0:T(4,128)} %bitcast.17, bf16[1,512,5120]{2,1,0:T(8,128)(2,1)} %feats_hbm.1, f32[1,5120]{1,0:T(1,128)} %bitcast.16, ...), custom_call_target="tpu_custom_call" | custom-call | tf_op jit(solution)/shard_map/pallas_call | solution.py:375
  49.1 0.7 %copy.16 = bf16[1,32,5120]{2,1,0:T(8,128)(2,1)} copy(bf16[1,32,5120]{2,1,0:T(8,128)(2,1)S(1)} %bitcast.11) | data formatting | bytes 655360
  49.9 0.7 %copy.17 = f32[1280,64]{0,1:T(8,128)} copy(f32[1280,64]{0,1:T(8,128)S(1)} %bitcast.10) | data formatting | bytes 655360
  50.6 0.6 %reduce = f32[1280]{0:T(1024)} reduce(f32[1,1280]{1,0:T(1,128)S(1)} %get-tuple-element.8, f32[]{:T(128)} %constant.4), dimensions={0}, to_apply=%get-tuple-element.8.reduce_sub_computation | reduce | bytes 10244 | tf_op jit(solution)/shard_map/pallas_call | solution.py:375

commit v6 on v5

--- a/solution.py
+++ b/solution.py
@@ -37,10 +37,10 @@
     qk_ref, fbuf, gain, gw, noise, ewin, hwin, ewin_s, hwin_s, wbuf,
     wpart, rx, wfull,
     ssq, x0, rms, xin, qbuf, kbuf, vext, obuf,
-    tsend, b1, b2, gfull, psend, crecv,
+    tsend, b1, gfull, psend, crecv,
     in_sem, feat_sem,
     s_rx, r_rx, s_ax, r_ax,
-    s_b1, r_b1, s_b2, r_b2, s_b3, r_b3, s_c, r_c, s_k, r_k,
+    s_b1, r_b1, s_b3, r_b3, s_c, r_c, s_k, r_k,
 ):
     L, S, X = sizes
     D = fbuf.shape[1]
@@ -59,16 +59,17 @@
     chips = Z * Y
     y, z = s // 4, lax.rem(s // 2, 2) * L + l
 
-    def chip(step_y, step_z):
-        to_y, to_z = lax.rem(y + step_y, Y), lax.rem(z + step_z, Z)
-        return {"level": lax.rem(to_z, L), "seq": 4 * to_y + 2 * (to_z // L) + core}
-
-    def around(steps_z):
-        steps = [(a, b) for a in range(Y) for b in steps_z if a or b]
+    def steps(steps_z):
         far = lambda step: min(step[0], Y - step[0]) + min(step[1], Z - step[1])
-        return [chip(*step) for step in sorted(steps, key=far, reverse=True)]
-
-    others = around(range(Z))
+        return sorted([(a, b) for a in range(Y) for b in steps_z if a or b], key=far, reverse=True)
+
+    def chip(step):
+        to_y, to_z = lax.rem(y + step[0], Y), lax.rem(z + step[1], Z)
+        return lax.rem(to_z, L), 4 * to_y + 2 * (to_z // L), to_z // L
+
+    def on_chip(step, of_core):
+        to_level, to_seq, z_hi = chip(step)
+        return {"level": to_level, "seq": to_seq + (z_hi if of_core is None else of_core)}
 
     def remote(src, dst, ssem, rsem, where):
         copy = pltpu.make_async_remote_copy(
@@ -81,7 +82,7 @@
         pltpu.make_async_copy(ref, ref, sem).wait()
 
     barrier = pltpu.get_barrier_semaphore()
-    for peer in others + team + [{"seq": mate}]:
+    for peer in [on_chip(step, c) for step in steps(range(Z)) for c in range(2)] + team + [{"seq": mate}]:
         pl.semaphore_signal(barrier, inc=1, device_id=peer, device_id_type=MESH)
 
     part = pin_hbm.shape[2]
@@ -188,7 +189,7 @@
     loads["gw"].wait()
     feat_chunk(0)
     feat_chunk(1)
-    pl.semaphore_wait(barrier, L * X + chips - 1)
+    pl.semaphore_wait(barrier, L * X - 1 + 2 * chips - 1)
     send_shares(0)
     send_shares(1)
     for c in range(2, FEAT_CHUNKS):
@@ -272,23 +273,29 @@
     def block_of(peer):
         return pl.ds(pl.multiple_of((peer["seq"] // 4 * L + peer["level"]) * trows, trows), trows)
 
-    me = {"level": l, "seq": s}
-    spot_b = s // 2 * L + l
-    b1[spot_b] = tsend[block_of(me), :]
-    for peer in others:
+    mine_b = block_of({"level": l, "seq": s})
+    owner = core == z // L
+    spot_b = 2 * (s // 2 * L + l) + core
+    for step in steps(range(Z)):
+        peer = on_chip(step, None)
         remote(tsend.at[block_of(peer)], b1.at[spot_b], s_b1, r_b1, peer)
-    drain(b1.at[pl.ds(0, chips - 1)], r_b1)
-    acc = b1[0].astype(F32)
-    for i in range(1, chips):
-        acc = acc + b1[i].astype(F32)
-    b2[core] = acc
-    remote(b2.at[core], b2.at[core], s_b2, r_b2, {"seq": mate})
-    drain(b2.at[0], r_b2)
-    mine_b = block_of(me)
-    gfull[mine_b, :] = (b2[0] + b2[1]).astype(BF)
-    for peer in around((0, 1, 2, Z - 1)):
-        remote(gfull.at[mine_b], gfull.at[mine_b], s_b3, r_b3, peer)
-    drain(b1.at[pl.ds(0, blocks - 1)], r_b3)
+
+    @pl.when(owner)
+    def _():
+        b1[spot_b] = tsend[mine_b, :]
+        drain(b1.at[pl.ds(0, 2 * chips - 1)], r_b1)
+        acc = b1[0].astype(F32)
+        for i in range(1, 2 * chips):
+            acc = acc + b1[i].astype(F32)
+        gfull[mine_b, :] = acc.astype(BF)
+        for peer in [on_chip(step, c) for step in steps((0, 1, 2, Z - 1)) for c in range(2)] + [{"seq": mate}]:
+            remote(gfull.at[mine_b], gfull.at[mine_b], s_b3, r_b3, peer)
+        drain(b1.at[pl.ds(0, blocks - 1)], r_b3)
+
+    @pl.when(jnp.logical_not(owner))
+    def _():
+        remote(tsend.at[mine_b], b1.at[spot_b], s_b1, r_b1, {"seq": mate})
+        drain(b1.at[pl.ds(0, blocks)], r_b3)
 
     cut = D // X
     side = cut // 2
@@ -334,8 +341,15 @@
         drain(rx.at[n], s_rx.at[n])
         drain(rx.at[n], s_ax.at[n])
     drain(b1.at[pl.ds(0, chips - 1)], s_b1)
-    drain(b2.at[0], s_b2)
-    drain(b1.at[pl.ds(0, blocks - 1)], s_b3)
+
+    @pl.when(owner)
+    def _():
+        drain(b1.at[pl.ds(0, 2 * blocks - 1)], s_b3)
+
+    @pl.when(jnp.logical_not(owner))
+    def _():
+        drain(b1.at[0], s_b1)
+
 
     drain(ow_ref.at[:, 0:side], r_k)
     block = pl.ds(pl.multiple_of(d * cut, 128), cut)
@@ -367,11 +381,10 @@
         V((2, 8 * chans, HD), BF), V((2, L * X - 1, 8 * chans // (L * X), HD), BF), V((2, 8 * chans, HD), BF),
         V((span, 128), F32), V((span, chans), F32), V((span, 128), F32), V((span, chans), BF),
         V((2, span, HD), BF), V((2, span, HD), BF), V((2, span, 2 * HD), BF), V((span, 2 * HD), BF),
-        V((half, 2 * chans), BF), V((L * S // 2, 4 * half // (L * S), 2 * chans), BF),
-        V((2, 4 * half // (L * S), 2 * chans), F32),
+        V((half, 2 * chans), BF), V((L * S, 4 * half // (L * S), 2 * chans), BF),
         V((half, 2 * chans), BF), V((X - 1, chans, side), BF), V((X, chans, side), BF),
         dma((12,)), dma((FEAT_CHUNKS,)),
-    ] + [dma((2,))] * 4 + [dma] * 10
+    ] + [dma((2,))] * 4 + [dma] * 8
     out_h, out_w, out_g = pl.pallas_call(
         functools.partial(kernel, sizes),
         out_shape=(

time: 51.3 us -> 50.8 us (level)
  no operation moved by 1% of the time
where the time goes in v6:
time: 50.8 us; the launch traced here: 50.7 us
  Pallas kernels  46.7 us (92%)
  between operations  1.93 us (4%)
  local copies, waits for them, and re-layouts  1.45 us (3%)
  other arithmetic  0.62 us (1%)
    pallas_call x1, Pallas kernels, on_device(): pl.pallas_call(functools.partial(kernel, sizes), out_shape=(V((rows_h, D)...  46.7 us
    unnamed x2, local copies, waits for them, and re-layouts  1.45 us

profile of v6, /device:TPU:1, one launch (start us, length us, event | category | flops | bytes accessed | tf_op | source)
XLA Modules:
  0.0 50.7 jit_solution(6915957134894402036)
XLA Ops:
  1.9 46.7 %shard_map.130 = (bf16[32,5120]{1,0:T(8,128)(2,1)S(1)}, f32[64,1280]{1,0:T(8,128)S(1)}, f32[1,1280]{1,0:T(1,128)S(1)}) custom-call(f32[1]{0:T(128)S(6)} %copy.18.sigma_ref, f32[1]{0:T(128)S(6)} %copy.19.lw_ref, f32[4,128]{1,0:T(4,128)} %bitcast.17, bf16[1,512,5120]{2,1,0:T(8,128)(2,1)} %feats_hbm.1, f32[1,5120]{1,0:T(1,128)} %bitcast.16, ...), custom_call_target="tpu_custom_call" | custom-call | tf_op jit(solution)/shard_map/pallas_call | solution.py:388
  48.7 0.7 %copy.16 = bf16[1,32,5120]{2,1,0:T(8,128)(2,1)} copy(bf16[1,32,5120]{2,1,0:T(8,128)(2,1)S(1)} %bitcast.11) | data formatting | bytes 655360
  49.4 0.7 %copy.17 = f32[1280,64]{0,1:T(8,128)} copy(f32[1280,64]{0,1:T(8,128)S(1)} %bitcast.10) | data formatting | bytes 655360
  50.1 0.6 %reduce = f32[1280]{0:T(1024)} reduce(f32[1,1280]{1,0:T(1,128)S(1)} %get-tuple-element.8, f32[]{:T(128)} %constant.4), dimensions={0}, to_apply=%get-tuple-element.8.reduce_sub_computation | reduce | bytes 10244 | tf_op jit(solution)/shard_map/pallas_call | solution.py:388

commit v7 on v6

--- a/solution.py
+++ b/solution.py
@@ -36,7 +36,7 @@
     oh_ref, ow_ref, og_ref,
     qk_ref, fbuf, gain, gw, noise, ewin, hwin, ewin_s, hwin_s, wbuf,
     wpart, rx, wfull,
-    ssq, x0, rms, xin, qbuf, kbuf, vext, obuf,
+    ssq, x0, rms, xin, qbuf, kbuf, pbuf, vext, obuf,
     tsend, b1, gfull, psend, crecv,
     in_sem, feat_sem,
     s_rx, r_rx, s_ax, r_ax,
@@ -128,16 +128,20 @@
         for n in range(2):
             for j in range(4):
                 wbuf[n, j, pad, :] = jnp.zeros((64, wbuf.shape[3]), BF)
-    for h in range(2):
-        vext[h, :, HD:] = jnp.ones((span, HD), BF)
+    for n in range(2):
+        for h in range(2):
+            vext[n, h, :, HD:] = jnp.ones((span, HD), BF)
+
+    def place(n, j):
+        return j // 2, (2 * n + j % 2) * 2 * chans
 
     def fuse(n):
         for j in range(4):
             left = ewin if j < 3 else hwin
             x = mm(left[n], wbuf[n, j]).astype(BF)
-            base = 2 * j * chans
-            wpart[n, base : base + chans, :] = x[:, :HD]
-            wpart[n, base + chans : base + 2 * chans, :] = x[:, HD:]
+            g, base = place(n, j)
+            wpart[g, base : base + chans, :] = x[:, :HD]
+            wpart[g, base + chans : base + 2 * chans, :] = x[:, HD:]
 
     share = 8 * chans // (L * X)
 
@@ -227,43 +231,46 @@
     total = packed(xin[...], bent)
 
     fold = math.log2(math.e) / math.sqrt(HD)
+    def matrix(n, j):
+        g, base = place(n, j)
+        return jnp.concatenate([wfull[g, base + h * chans : base + (h + 1) * chans] for h in range(2)], axis=1)
+
+    def active(rows, mat):
+        a = mm(xin[rows, :], mat) * 0.5
+        return a * jnp.tanh(a) + a
+
+    drain(rx.at[0], r_ax.at[0])
     for n in range(2):
-        drain(rx.at[n], r_ax.at[n])
-        mats = [
-            jnp.concatenate([wfull[n, (2 * j + h) * chans : (2 * j + h + 1) * chans] for h in range(2)], axis=1)
-            for j in range(4)
-        ]
-
-        def rows_body(i, _, n=n, mats=mats):
-            rows = pl.ds(pl.multiple_of(i * 128, 128), 128)
-            x = xin[rows, :]
-            for j in range(3):
-                a = mm(x, mats[j]) * 0.5
-                act = a * jnp.tanh(a) + a
+        for j, buf in enumerate((qbuf, kbuf)):
+            mat = matrix(n, j)
+            row = qk_ref[2 * n + j : 2 * n + j + 1, :]
+            if j == 0:
+                row = row * fold
+            for i in range(span // 128):
+                rows = slice(i * 128, (i + 1) * 128)
+                act = active(rows, mat)
                 for h in range(2):
                     t = act[:, h * HD : (h + 1) * HD]
-                    if j == 2:
-                        vext[h, rows, 0:HD] = t.astype(BF)
-                        continue
                     mean = jnp.mean(t * t, axis=-1, keepdims=True)
-                    row = qk_ref[2 * n + j : 2 * n + j + 1, :]
-                    if j == 0:
-                        row = row * fold
-                    t = (t * lax.rsqrt(mean + 1e-06) * row).astype(BF)
-                    if j == 0:
-                        qbuf[h, rows, :] = t
-                    else:
-                        kbuf[h, rows, :] = t
-            return 0
-
-        lax.fori_loop(0, span // 128, rows_body, 0, unroll=True)
+                    buf[n, h, rows, :] = (t * lax.rsqrt(mean + 1e-06) * row).astype(BF)
         for b in range(span // QBLOCK):
             rows = slice(b * QBLOCK, (b + 1) * QBLOCK)
             for h in range(2):
-                weights = jnp.exp2(mm(qbuf[h, rows, :], kbuf[h], NT)).astype(BF)
-                both = mm(weights, vext[h])
-                obuf[rows, h * HD : (h + 1) * HD] = (both[:, :HD] / both[:, HD:]).astype(BF)
-        field = packed(obuf[...], mats[3])
+                pbuf[n, h, rows, :] = jnp.exp2(mm(qbuf[n, h, rows, :], kbuf[n, h], NT)).astype(BF)
+    drain(rx.at[1], r_ax.at[1])
+    for n in range(2):
+        mat = matrix(n, 2)
+        for i in range(span // 128):
+            rows = slice(i * 128, (i + 1) * 128)
+            act = active(rows, mat)
+            for h in range(2):
+                vext[n, h, rows, 0:HD] = act[:, h * HD : (h + 1) * HD].astype(BF)
+        for b in range(span // QBLOCK):
+            rows = slice(b * QBLOCK, (b + 1) * QBLOCK)
+            for h in range(2):
+                both = mm(pbuf[n, h, rows, :], vext[n, h])
+                obuf[n, rows, h * HD : (h + 1) * HD] = (both[:, :HD] / both[:, HD:]).astype(BF)
+        field = packed(obuf[n], matrix(n, 3))
         total = total + field if n else total - field
 
     tsend[...] = (total * lw_ref[0]).astype(BF)
@@ -380,7 +387,8 @@
         V((2, 4, win_a, 2 * HD), BF),
         V((2, 8 * chans, HD), BF), V((2, L * X - 1, 8 * chans // (L * X), HD), BF), V((2, 8 * chans, HD), BF),
         V((span, 128), F32), V((span, chans), F32), V((span, 128), F32), V((span, chans), BF),
-        V((2, span, HD), BF), V((2, span, HD), BF), V((2, span, 2 * HD), BF), V((span, 2 * HD), BF),
+        V((2, 2, span, HD), BF), V((2, 2, span, HD), BF), V((2, 2, span, span), BF),
+        V((2, 2, span, 2 * HD), BF), V((2, span, 2 * HD), BF),
         V((half, 2 * chans), BF), V((L * S, 4 * half // (L * S), 2 * chans), BF),
         V((half, 2 * chans), BF), V((X - 1, chans, side), BF), V((X, chans, side), BF),
         dma((12,)), dma((FEAT_CHUNKS,)),

time: 50.8 us -> 50.7 us (level)
  no operation moved by 1% of the time
where the time goes in v7:
time: 50.7 us; the launch traced here: 50.6 us
  Pallas kernels  46.6 us (92%)
  between operations  1.93 us (4%)
  local copies, waits for them, and re-layouts  1.45 us (3%)
  other arithmetic  0.62 us (1%)
    pallas_call x1, Pallas kernels, on_device(): pl.pallas_call(functools.partial(kernel, sizes), out_shape=(V((rows_h, D)...  46.6 us
    unnamed x2, local copies, waits for them, and re-layouts  1.45 us

profile of v7, /device:TPU:1, one launch (start us, length us, event | category | flops | bytes accessed | tf_op | source)
XLA Modules:
  0.0 50.6 jit_solution(11217056408497593660)
XLA Ops:
  1.9 46.6 %shard_map.130 = (bf16[32,5120]{1,0:T(8,128)(2,1)S(1)}, f32[64,1280]{1,0:T(8,128)S(1)}, f32[1,1280]{1,0:T(1,128)S(1)}) custom-call(f32[1]{0:T(128)S(6)} %copy.18.sigma_ref, f32[1]{0:T(128)S(6)} %copy.19.lw_ref, f32[4,128]{1,0:T(4,128)} %bitcast.17, bf16[1,512,5120]{2,1,0:T(8,128)(2,1)} %feats_hbm.1, f32[1,5120]{1,0:T(1,128)} %bitcast.16, ...), custom_call_target="tpu_custom_call" | custom-call | tf_op jit(solution)/shard_map/pallas_call | solution.py:396
  48.5 0.7 %copy.16 = bf16[1,32,5120]{2,1,0:T(8,128)(2,1)} copy(bf16[1,32,5120]{2,1,0:T(8,128)(2,1)S(1)} %bitcast.11) | data formatting | bytes 655360
  49.3 0.7 %copy.17 = f32[1280,64]{0,1:T(8,128)} copy(f32[1280,64]{0,1:T(8,128)S(1)} %bitcast.10) | data formatting | bytes 655360
  50.0 0.6 %reduce = f32[1280]{0:T(1024)} reduce(f32[1,1280]{1,0:T(1,128)S(1)} %get-tuple-element.8, f32[]{:T(128)} %constant.4), dimensions={0}, to_apply=%get-tuple-element.8.reduce_sub_computation | reduce | bytes 10244 | tf_op jit(solution)/shard_map/pallas_call | solution.py:396

commit v8 on v7

--- a/solution.py
+++ b/solution.py
@@ -55,6 +55,7 @@
     team = [
         {"level": mirror[a], "dp": lax.rem(d + b, X)} for a in (3, 2, 1, 0) for b in (2, 1, 3, 0) if a or b
     ]
+    away = [{"level": mirror[a], "dp": lax.rem(d + b, X)} for a in (3, 2, 1, 0) for b in (2, 1, 3)]
     Z, Y = 2 * L, S // 4
     chips = Z * Y
     y, z = s // 4, lax.rem(s // 2, 2) * L + l
@@ -82,7 +83,7 @@
         pltpu.make_async_copy(ref, ref, sem).wait()
 
     barrier = pltpu.get_barrier_semaphore()
-    for peer in [on_chip(step, c) for step in steps(range(Z)) for c in range(2)] + team + [{"seq": mate}]:
+    for peer in [on_chip(step, c) for step in steps(range(Z)) for c in range(2)] + away + [{"seq": mate}]:
         pl.semaphore_signal(barrier, inc=1, device_id=peer, device_id_type=MESH)
 
     part = pin_hbm.shape[2]
@@ -193,7 +194,7 @@
     loads["gw"].wait()
     feat_chunk(0)
     feat_chunk(1)
-    pl.semaphore_wait(barrier, L * X - 1 + 2 * chips - 1)
+    pl.semaphore_wait(barrier, L * (X - 1) + 2 * chips - 1)
     send_shares(0)
     send_shares(1)
     for c in range(2, FEAT_CHUNKS):
@@ -361,7 +362,7 @@
     drain(ow_ref.at[:, 0:side], r_k)
     block = pl.ds(pl.multiple_of(d * cut, 128), cut)
     inside = jnp.sum(ow_ref[...] * gw[:, block].astype(F32), axis=0, keepdims=True)
-    og_ref[...] = inside / gain[:, block]
+    og_ref[...] = (inside / gain[:, block])[0]
     drain(ow_ref.at[:, 0:side], s_k)
 
 
@@ -398,7 +399,7 @@
         out_shape=(
             V((rows_h, D), BF),
             V((chans, 2 * side), F32),
-            V((1, 2 * side), F32),
+            V((2 * side,), F32),
         ),
         in_specs=[smem] * 2 + [hbm] * 9,
         out_specs=(vmem, vmem, vmem),
@@ -417,7 +418,7 @@
             )
         ),
     )
-    return out_h[None], out_w.T, out_g[0]
+    return out_h[None], out_w.T, out_g
 
 
 def solution(mesh):

time: 50.7 us -> 50.7 us (level)
  other arithmetic: 0.62 us -> 0 us
  local copies, waits for them, and re-layouts: 1.45 us -> 2.05 us
    pallas_call x1 -> x0, other arithmetic: 0.62 us -> none  [on_device(): pl.pallas_call(functools.partial(kernel, sizes), out_shape=(V((rows_h, D)...]
    unnamed x2 -> x3, local copies, waits for them, and re-layouts: 1.45 us -> 2.05 us
where the time goes in v8:
time: 50.7 us; the launch traced here: 50.6 us
  Pallas kernels  46.6 us (92%)
  local copies, waits for them, and re-layouts  2.05 us (4%)
  between operations  1.93 us (4%)
    pallas_call x1, Pallas kernels, on_device(): pl.pallas_call(functools.partial(kernel, sizes), out_shape=(V((rows_h, D)...  46.6 us
    unnamed x3, local copies, waits for them, and re-layouts  2.05 us

profile of v8, /device:TPU:1, one launch (start us, length us, event | category | flops | bytes accessed | tf_op | source)
XLA Modules:
  0.0 50.6 jit_solution(9462414010339126578)
XLA Ops:
  1.9 46.6 %shard_map.130 = (bf16[32,5120]{1,0:T(8,128)(2,1)S(1)}, f32[64,1280]{1,0:T(8,128)S(1)}, f32[1280]{0:T(1024)S(1)}) custom-call(f32[1]{0:T(128)S(6)} %copy.20.sigma_ref, f32[1]{0:T(128)S(6)} %copy.21.lw_ref, f32[4,128]{1,0:T(4,128)} %bitcast.17, bf16[1,512,5120]{2,1,0:T(8,128)(2,1)} %feats_hbm.1, f32[1,5120]{1,0:T(1,128)} %bitcast.16, ...), custom_call_target="tpu_custom_call" | custom-call | tf_op jit(solution)/shard_map/pallas_call | solution.py:397
  48.5 0.7 %copy.17 = bf16[1,32,5120]{2,1,0:T(8,128)(2,1)} copy(bf16[1,32,5120]{2,1,0:T(8,128)(2,1)S(1)} %bitcast.11) | data formatting | bytes 655360
  49.3 0.7 %copy.18 = f32[1280,64]{0,1:T(8,128)} copy(f32[1280,64]{0,1:T(8,128)S(1)} %bitcast.10) | data formatting | bytes 655360
  50.0 0.6 %copy.19 = f32[1280]{0:T(1024)} copy(f32[1280]{0:T(1024)S(1)} %get-tuple-element.11) | data formatting | bytes 10240

commit v9 on v8

--- a/solution.py
+++ b/solution.py
@@ -178,7 +178,7 @@
             ssq[rows, :] = acc if c == 0 else ssq[rows, :] + acc
             return 0
 
-        lax.fori_loop(0, span // 64, rows_body, 0)
+        lax.fori_loop(0, span // 64, rows_body, 0, unroll=True)
         prod = mm(fbuf[:, c * fc : (c + 1) * fc], scaled, NT)
         x0[...] = prod if c == 0 else x0[...] + prod
 

time: 50.7 us -> 51.1 us (level)
  no operation moved by 1% of the time
where the time goes in v9:
time: 51.1 us; the launch traced here: 51 us
  Pallas kernels  47 us (92%)
  local copies, waits for them, and re-layouts  2.05 us (4%)
  between operations  1.93 us (4%)
    pallas_call x1, Pallas kernels, on_device(): pl.pallas_call(functools.partial(kernel, sizes), out_shape=(V((rows_h, D)...  47 us
    unnamed x3, local copies, waits for them, and re-layouts  2.05 us

profile of v9, /device:TPU:1, one launch (start us, length us, event | category | flops | bytes accessed | tf_op | source)
XLA Modules:
  0.0 51.0 jit_solution(17386946658286078897)
XLA Ops:
  1.9 47.0 %shard_map.130 = (bf16[32,5120]{1,0:T(8,128)(2,1)S(1)}, f32[64,1280]{1,0:T(8,128)S(1)}, f32[1280]{0:T(1024)S(1)}) custom-call(f32[1]{0:T(128)S(6)} %copy.20.sigma_ref, f32[1]{0:T(128)S(6)} %copy.21.lw_ref, f32[4,128]{1,0:T(4,128)} %bitcast.17, bf16[1,512,5120]{2,1,0:T(8,128)(2,1)} %feats_hbm.1, f32[1,5120]{1,0:T(1,128)} %bitcast.16, ...), custom_call_target="tpu_custom_call" | custom-call | tf_op jit(solution)/shard_map/pallas_call | solution.py:397
  48.9 0.7 %copy.17 = bf16[1,32,5120]{2,1,0:T(8,128)(2,1)} copy(bf16[1,32,5120]{2,1,0:T(8,128)(2,1)S(1)} %bitcast.11) | data formatting | bytes 655360
  49.6 0.7 %copy.18 = f32[1280,64]{0,1:T(8,128)} copy(f32[1280,64]{0,1:T(8,128)S(1)} %bitcast.10) | data formatting | bytes 655360
  50.4 0.6 %copy.19 = f32[1280]{0:T(1024)} copy(f32[1280]{0:T(1024)S(1)} %get-tuple-element.11) | data formatting | bytes 10240
